TPU v7x, 32 devices: a whole 2x2x4 slice. The times are simulated.
32 devices in a mesh: fsdp: 8 (over y, x, core), ctx: 2 (over z_hi), tp: 2 (over z_lo).
Axes of the slice: x: 2, y: 2, z: 4 (z_hi: 2, z_lo: 2; z = z_hi * 2 + z_lo), core: 2. Of those that a mesh axis runs over, the one named last changes fastest.
Arguments:
- tokens: bfloat16 [8, 320, 1024], P('fsdp', 'ctx'), may hold values from -6 to 6
- lengths: int32 [8], P('fsdp'), may hold values from 0 to 320, as said below
- cotangent: bfloat16 [8, 320, 1024], P('fsdp', 'ctx'), may hold values from -6 to 6
- attn_gain: bfloat16 [3, 1024], P(None, ('fsdp', 'ctx')), may hold values from 0.5 to 1.5
- attn_shift: bfloat16 [3, 1024], P(None, ('fsdp', 'ctx')), may hold values from -1.75 to 1.75
- qkv_weight: bfloat16 [3, 1024, 3, 1024], P(None, ('fsdp', 'ctx'), None, 'tp'), may hold values from -0.1875 to 0.1875
- qv_bias: bfloat16 [3, 2, 1024], P(None, None, 'tp'), may hold values from -3 to 3
- out_weight: bfloat16 [3, 1024, 1024], P(None, 'tp', ('fsdp', 'ctx')), may hold values from -0.1875 to 0.1875
- out_bias: bfloat16 [3, 1024], P(None, ('fsdp', 'ctx')), may hold values from -1.75 to 1.75
- mlp_gain: bfloat16 [3, 1024], P(None, ('fsdp', 'ctx')), may hold values from 0.5 to 1.5
- mlp_shift: bfloat16 [3, 1024], P(None, ('fsdp', 'ctx')), may hold values from -1.75 to 1.75
- up_weight: bfloat16 [3, 1024, 4096], P(None, ('fsdp', 'ctx'), 'tp'), may hold values from -0.1875 to 0.1875
- up_bias: bfloat16 [3, 4096], P(None, 'tp'), may hold values from -3 to 3
- down_weight: bfloat16 [3, 4096, 1024], P(None, 'tp', ('fsdp', 'ctx')), may hold values from -0.09375 to 0.09375
- down_bias: bfloat16 [3, 1024], P(None, ('fsdp', 'ctx')), may hold values from -1.75 to 1.75
Outputs:
- output: bfloat16 [8, 320, 1024], P('fsdp', 'ctx')
- input_grad: float32 [8, 320, 1024], P('fsdp', 'ctx')
- grad_attn_gain: float32 [3, 1024], P(None, ('fsdp', 'ctx'))
- grad_attn_shift: float32 [3, 1024], P(None, ('fsdp', 'ctx'))
- grad_qkv_weight: float32 [3, 1024, 3, 1024], P(None, ('fsdp', 'ctx'), None, 'tp')
- grad_qv_bias: float32 [3, 2, 1024], P(None, None, 'tp')
- grad_out_weight: float32 [3, 1024, 1024], P(None, 'tp', ('fsdp', 'ctx'))
- grad_out_bias: float32 [3, 1024], P(None, ('fsdp', 'ctx'))
- grad_mlp_gain: float32 [3, 1024], P(None, ('fsdp', 'ctx'))
- grad_mlp_shift: float32 [3, 1024], P(None, ('fsdp', 'ctx'))
- grad_up_weight: float32 [3, 1024, 4096], P(None, ('fsdp', 'ctx'), 'tp')
- grad_up_bias: float32 [3, 4096], P(None, 'tp')
- grad_down_weight: float32 [3, 4096, 1024], P(None, 'tp', ('fsdp', 'ctx'))
- grad_down_bias: float32 [3, 1024], P(None, ('fsdp', 'ctx'))
Inputs may be any that keep to these rules, and one draw needn't show every extreme that they name: `lengths`: image places 1 * g to 1 * g + 1 - 1 form group g; in each group the first 1 to 1 places hold live images of length 224 to 320, the others have length 0; some image has length 320 and some group is full.
All inputs are finite; a program needn't handle non-finite values.
Results may differ from a plain program's by a relative error of at most 0.012.
Values may be sent and summed in bfloat16 or wider, within the bound.
A program may use at most 256 MiB of HBM per device.

v0:
```python
import jax
import jax.numpy as jnp
from jax import lax
from jax.sharding import PartitionSpec as P

HEAD_DIM = 64


EPS = 1e-05
NEG = -30000.0


def layer_norm(values, norm_gain, norm_shift):
    row_mean = jnp.mean(values, axis=-1, keepdims=True)
    centered = values - row_mean
    row_var = jnp.mean(centered * centered, axis=-1, keepdims=True)
    return centered * lax.rsqrt(row_var + EPS) * norm_gain + norm_shift


def gelu_exact(values):
    return jax.nn.gelu(values, approximate=False)


def head_sum(partial_rows):
    return lax.psum(partial_rows, "tp")


def fetch_weights(gain_a, shift_a, qkv_w, out_w, out_b, gain_b, shift_b, up_w, down_w, down_b):
    return (
        lax.all_gather(gain_a, ("fsdp", "ctx"), axis=0, tiled=True),
        lax.all_gather(shift_a, ("fsdp", "ctx"), axis=0, tiled=True),
        lax.all_gather(qkv_w, ("fsdp", "ctx"), axis=0, tiled=True),
        lax.all_gather(out_w, ("fsdp", "ctx"), axis=1, tiled=True),
        lax.all_gather(out_b, ("fsdp", "ctx"), axis=0, tiled=True),
        lax.all_gather(gain_b, ("fsdp", "ctx"), axis=0, tiled=True),
        lax.all_gather(shift_b, ("fsdp", "ctx"), axis=0, tiled=True),
        lax.all_gather(up_w, ("fsdp", "ctx"), axis=0, tiled=True),
        lax.all_gather(down_w, ("fsdp", "ctx"), axis=1, tiled=True),
        lax.all_gather(down_b, ("fsdp", "ctx"), axis=0, tiled=True),
    )


def fetch_again(gain_a, shift_a, qkv_w, out_w, out_b, gain_b, shift_b, up_w, down_w, down_b):
    return (
        lax.all_gather(gain_a, ("fsdp", "ctx"), axis=0, tiled=True),
        lax.all_gather(shift_a, ("fsdp", "ctx"), axis=0, tiled=True),
        lax.all_gather(qkv_w, ("fsdp", "ctx"), axis=0, tiled=True),
        lax.all_gather(out_w, ("fsdp", "ctx"), axis=1, tiled=True),
        lax.all_gather(out_b, ("fsdp", "ctx"), axis=0, tiled=True),
        lax.all_gather(gain_b, ("fsdp", "ctx"), axis=0, tiled=True),
        lax.all_gather(shift_b, ("fsdp", "ctx"), axis=0, tiled=True),
        lax.all_gather(up_w, ("fsdp", "ctx"), axis=0, tiled=True),
        lax.all_gather(down_w, ("fsdp", "ctx"), axis=1, tiled=True),
        lax.all_gather(down_b, ("fsdp", "ctx"), axis=0, tiled=True),
    )


def masked_scores(query_heads, key_heads, key_live, score_scale):
    raw_scores = (
        jnp.einsum("nqhd,nkhd->nhqk", query_heads, key_heads, preferred_element_type=jnp.float32)
        * score_scale
    )
    return jnp.where(key_live, raw_scores, NEG)


def body(
    tokens,
    lengths,
    cotangent,
    attn_gain,
    attn_shift,
    qkv_weight,
    qv_bias,
    out_weight,
    out_bias,
    mlp_gain,
    mlp_shift,
    up_weight,
    up_bias,
    down_weight,
    down_bias,
):
    images, local_slots, model_width = tokens.shape
    slots_all = local_slots * lax.axis_size("ctx")
    layers = qkv_weight.shape[0]
    heads_here = qkv_weight.shape[3] // HEAD_DIM
    score_scale = HEAD_DIM ** (-0.5)
    slot_ids = lax.axis_index("ctx") * local_slots + jnp.arange(local_slots, dtype=jnp.int32)
    row_mask = (slot_ids[None, :] < lengths[:, None]).astype(jnp.float32)[:, :, None]
    key_live = (jnp.arange(slots_all, dtype=jnp.int32)[None, :] < lengths[:, None])[
        :, None, None, :
    ]
    stream = tokens.astype(jnp.float32) * row_mask
    kept = []
    for layer_index in range(layers):
        fetched = fetch_weights(
            attn_gain[layer_index],
            attn_shift[layer_index],
            qkv_weight[layer_index],
            out_weight[layer_index],
            out_bias[layer_index],
            mlp_gain[layer_index],
            mlp_shift[layer_index],
            up_weight[layer_index],
            down_weight[layer_index],
            down_bias[layer_index],
        )
        gain_a, shift_a, qkv_w, out_w, out_b, gain_b, shift_b, up_w, down_w, down_b = fetched
        normed_a = layer_norm(
            stream, gain_a.astype(jnp.float32), shift_a.astype(jnp.float32)
        ).astype(jnp.bfloat16)
        projected = jnp.einsum("nsd,dtf->nstf", normed_a, qkv_w, preferred_element_type=jnp.float32)
        bias_qv = qv_bias[layer_index].astype(jnp.float32)
        queries = (projected[:, :, 0] + bias_qv[0]).astype(jnp.bfloat16)
        keys_own = projected[:, :, 1].astype(jnp.bfloat16)
        values_own = (projected[:, :, 2] + bias_qv[1]).astype(jnp.bfloat16)
        keys_all, values_all = (
            lax.all_gather(keys_own, "ctx", axis=1, tiled=True),
            lax.all_gather(values_own, "ctx", axis=1, tiled=True),
        )
        query_heads = queries.reshape(images, local_slots, heads_here, HEAD_DIM)
        key_heads = keys_all.reshape(images, slots_all, heads_here, HEAD_DIM)
        value_heads = values_all.reshape(images, slots_all, heads_here, HEAD_DIM)
        scores = masked_scores(query_heads, key_heads, key_live, score_scale)
        row_top = jnp.max(scores, axis=-1, keepdims=True)
        exp_scores = jnp.exp(scores - row_top)
        row_total = jnp.sum(exp_scores, axis=-1, keepdims=True)
        attn_probs = (exp_scores / row_total).astype(jnp.bfloat16)
        log_total = row_top + jnp.log(row_total)
        attended = jnp.einsum(
            "nhqk,nkhd->nqhd", attn_probs, value_heads, preferred_element_type=jnp.float32
        )
        attended = attended.reshape(images, local_slots, heads_here * HEAD_DIM).astype(jnp.bfloat16)
        branch_a = head_sum(
            jnp.einsum("nsf,fd->nsd", attended, out_w, preferred_element_type=jnp.float32)
        )
        mid = stream + row_mask * (branch_a + out_b.astype(jnp.float32))
        normed_b = layer_norm(mid, gain_b.astype(jnp.float32), shift_b.astype(jnp.float32)).astype(
            jnp.bfloat16
        )
        hidden_pre = jnp.einsum(
            "nsd,df->nsf", normed_b, up_w, preferred_element_type=jnp.float32
        ) + up_bias[layer_index].astype(jnp.float32)
        hidden = gelu_exact(hidden_pre).astype(jnp.bfloat16)
        branch_b = head_sum(
            jnp.einsum("nsf,fd->nsd", hidden, down_w, preferred_element_type=jnp.float32)
        )
        kept.append(
            (
                stream,
                normed_a,
                query_heads,
                key_heads,
                value_heads,
                log_total,
                attended,
                mid,
                normed_b,
                hidden_pre,
                hidden,
                fetched,
            )
        )
        stream = mid + row_mask * (branch_b + down_b.astype(jnp.float32))
    output = stream.astype(jnp.bfloat16)
    grad_stream = cotangent.astype(jnp.float32)
    weight_sums = [None] * layers
    bias_sums = [None] * layers
    for layer_index in reversed(range(layers)):
        (
            layer_in,
            normed_a,
            query_heads,
            key_heads,
            value_heads,
            log_total,
            attended,
            mid,
            normed_b,
            hidden_pre,
            hidden,
            fetched,
        ) = kept[layer_index]
        weights_now = fetch_again(
            attn_gain[layer_index],
            attn_shift[layer_index],
            qkv_weight[layer_index],
            out_weight[layer_index],
            out_bias[layer_index],
            mlp_gain[layer_index],
            mlp_shift[layer_index],
            up_weight[layer_index],
            down_weight[layer_index],
            down_bias[layer_index],
        )
        gain_a, shift_a, qkv_w, out_w, out_b, gain_b, shift_b, up_w, down_w, down_b = weights_now
        grad_branch_b = row_mask * grad_stream
        grad_down_b = jnp.sum(grad_branch_b, axis=(0, 1))
        low_b = grad_branch_b.astype(jnp.bfloat16)
        grad_down_w = jnp.einsum("nsf,nsd->fd", hidden, low_b, preferred_element_type=jnp.float32)
        grad_hidden = jnp.einsum("nsd,fd->nsf", low_b, down_w, preferred_element_type=jnp.float32)
        grad_pre = jax.vjp(gelu_exact, hidden_pre)[1](grad_hidden)[0]
        grad_up_b = jnp.sum(grad_pre, axis=(0, 1))
        low_pre = grad_pre.astype(jnp.bfloat16)
        grad_up_w = jnp.einsum("nsd,nsf->df", normed_b, low_pre, preferred_element_type=jnp.float32)
        grad_normed_b = head_sum(
            jnp.einsum("nsf,df->nsd", low_pre, up_w, preferred_element_type=jnp.float32)
        )
        pull_mid = jax.vjp(
            layer_norm, mid, gain_b.astype(jnp.float32), shift_b.astype(jnp.float32)
        )[1]
        grad_mid_norm, grad_gain_b, grad_shift_b = pull_mid(grad_normed_b)
        grad_mid = grad_stream + grad_mid_norm
        grad_branch_a = row_mask * grad_mid
        grad_out_b = jnp.sum(grad_branch_a, axis=(0, 1))
        low_a = grad_branch_a.astype(jnp.bfloat16)
        grad_out_w = jnp.einsum("nsf,nsd->fd", attended, low_a, preferred_element_type=jnp.float32)
        grad_att = jnp.einsum(
            "nsd,fd->nsf", low_a, out_w, preferred_element_type=jnp.float32
        ).astype(jnp.bfloat16)
        grad_att = grad_att.reshape(images, local_slots, heads_here, HEAD_DIM)
        scores = masked_scores(query_heads, key_heads, key_live, score_scale)
        attn_p = jnp.exp(scores - log_total)
        grad_probs = jnp.einsum(
            "nqhd,nkhd->nhqk", grad_att, value_heads, preferred_element_type=jnp.float32
        )
        row_dot = jnp.sum(attn_p * grad_probs, axis=-1, keepdims=True)
        grad_scores = (attn_p * (grad_probs - row_dot)).astype(jnp.bfloat16)
        grad_q = (
            jnp.einsum(
                "nhqk,nkhd->nqhd", grad_scores, key_heads, preferred_element_type=jnp.float32
            )
            * score_scale
        ).astype(jnp.bfloat16)
        grad_q = grad_q.reshape(images, local_slots, heads_here * HEAD_DIM)
        grad_k_all = (
            jnp.einsum(
                "nhqk,nqhd->nkhd", grad_scores, query_heads, preferred_element_type=jnp.float32
            )
            * score_scale
        )
        grad_v_all = jnp.einsum(
            "nhqk,nqhd->nkhd",
            attn_p.astype(jnp.bfloat16),
            grad_att,
            preferred_element_type=jnp.float32,
        )
        grad_k_all = grad_k_all.reshape(images, slots_all, heads_here * HEAD_DIM)
        grad_v_all = grad_v_all.reshape(images, slots_all, heads_here * HEAD_DIM)
        grad_k, grad_v = (
            lax.psum_scatter(grad_k_all, "ctx", scatter_dimension=1, tiled=True),
            lax.psum_scatter(grad_v_all, "ctx", scatter_dimension=1, tiled=True),
        )
        grad_k = grad_k.astype(jnp.bfloat16)
        grad_v = grad_v.astype(jnp.bfloat16)
        grad_qkv = jnp.stack((grad_q, grad_k, grad_v), axis=2)
        grad_qv_b = jnp.stack(
            (
                jnp.sum(grad_q.astype(jnp.float32), axis=(0, 1)),
                jnp.sum(grad_v.astype(jnp.float32), axis=(0, 1)),
            )
        )
        grad_qkv_w = jnp.einsum(
            "nsd,nstf->dtf", normed_a, grad_qkv, preferred_element_type=jnp.float32
        )
        grad_normed_a = head_sum(
            jnp.einsum("nstf,dtf->nsd", grad_qkv, qkv_w, preferred_element_type=jnp.float32)
        )
        pull_in = jax.vjp(
            layer_norm, layer_in, gain_a.astype(jnp.float32), shift_a.astype(jnp.float32)
        )[1]
        grad_in_norm, grad_gain_a, grad_shift_a = pull_in(grad_normed_a)
        grad_stream = grad_mid + grad_in_norm
        layer_grads = (
            grad_gain_a,
            grad_shift_a,
            grad_qkv_w,
            grad_out_w,
            grad_out_b,
            grad_gain_b,
            grad_shift_b,
            grad_up_w,
            grad_down_w,
            grad_down_b,
        )
        weight_sums[layer_index] = (
            lax.psum_scatter(layer_grads[0], ("fsdp", "ctx"), scatter_dimension=0, tiled=True),
            lax.psum_scatter(layer_grads[1], ("fsdp", "ctx"), scatter_dimension=0, tiled=True),
            lax.psum_scatter(layer_grads[2], ("fsdp", "ctx"), scatter_dimension=0, tiled=True),
            lax.psum_scatter(layer_grads[3], ("fsdp", "ctx"), scatter_dimension=1, tiled=True),
            lax.psum_scatter(layer_grads[4], ("fsdp", "ctx"), scatter_dimension=0, tiled=True),
            lax.psum_scatter(layer_grads[5], ("fsdp", "ctx"), scatter_dimension=0, tiled=True),
            lax.psum_scatter(layer_grads[6], ("fsdp", "ctx"), scatter_dimension=0, tiled=True),
            lax.psum_scatter(layer_grads[7], ("fsdp", "ctx"), scatter_dimension=0, tiled=True),
            lax.psum_scatter(layer_grads[8], ("fsdp", "ctx"), scatter_dimension=1, tiled=True),
            lax.psum_scatter(layer_grads[9], ("fsdp", "ctx"), scatter_dimension=0, tiled=True),
        )
        bias_sums[layer_index] = lax.psum((grad_qv_b, grad_up_b), ("fsdp", "ctx"))
    input_grad = grad_stream * row_mask

    def stacked(member, source):
        return jnp.stack([entry[member] for entry in source], axis=0)

    summed = tuple((stacked(member, weight_sums) for member in range(10)))
    return (
        output,
        input_grad,
        summed[0],
        summed[1],
        summed[2],
        stacked(0, bias_sums),
        summed[3],
        summed[4],
        summed[5],
        summed[6],
        summed[7],
        stacked(1, bias_sums),
        summed[8],
        summed[9],
    )


def solution(mesh):
    return jax.shard_map(
        body,
        mesh=mesh,
        in_specs=(
            P("fsdp", "ctx", None),
            P("fsdp"),
            P("fsdp", "ctx", None),
            P(None, ("fsdp", "ctx")),
            P(None, ("fsdp", "ctx")),
            P(None, ("fsdp", "ctx"), None, "tp"),
            P(None, None, "tp"),
            P(None, "tp", ("fsdp", "ctx")),
            P(None, ("fsdp", "ctx")),
            P(None, ("fsdp", "ctx")),
            P(None, ("fsdp", "ctx")),
            P(None, ("fsdp", "ctx"), "tp"),
            P(None, "tp"),
            P(None, "tp", ("fsdp", "ctx")),
            P(None, ("fsdp", "ctx")),
        ),
        out_specs=(
            P("fsdp", "ctx", None),
            P("fsdp", "ctx", None),
            P(None, ("fsdp", "ctx")),
            P(None, ("fsdp", "ctx")),
            P(None, ("fsdp", "ctx"), None, "tp"),
            P(None, None, "tp"),
            P(None, "tp", ("fsdp", "ctx")),
            P(None, ("fsdp", "ctx")),
            P(None, ("fsdp", "ctx")),
            P(None, ("fsdp", "ctx")),
            P(None, ("fsdp", "ctx"), "tp"),
            P(None, "tp"),
            P(None, "tp", ("fsdp", "ctx")),
            P(None, ("fsdp", "ctx")),
        ),
        check_vma=False,
    )
```

profile of v0, /device:TPU:0, one launch (start us, length us, event | category | flops | bytes accessed | tf_op | source)
XLA Modules:
  0.0 4591.7 jit_solution(13190257869893100468)
XLA Ops:
  16.6 64.4 %all-reduce.38 = (bf16[1024]{0:T(1024)(128)(2,1)S(1)}, bf16[1024]{0:T(1024)(128)(2,1)S(1)}, bf16[1024]{0:T(1024)(128)(2,1)S(1)}, bf16[1024]{0:T(1024)(128)(2,1)S...) all-reduce(bf16[1024]{0:T(1024)(128)(2,1)S(1)} %dynamic-update-slic, ...), channel_id=3, replica_groups=mesh['fsdp'=8,'ctx'=2,'tp'=2] {'fsdp','ctx'}, use_global_device_ids=true, to_apply=%add.1 | all-reduce | flops 18432 | bytes 73728
  118.4 28.1 all-reduce.52.cloned.1.call-done
  148.2 56.5 %all-gather.50.cloned.1.call-done = bf16[1,1024,2048]{2,1,0:T(8,128)(2,1)} async-done(((bf16[1,64,2048]{2,1,0:T(8,128)(2,1)}), bf16[1,1024,2048]{2,1,0:T(8,128)(2,1)}) %all-gather.50.cloned.1.call-update) | async-done | bytes 4194320 | tf_op jit(solution)/shard_map/all_gather | solution.py:37
  211.6 50.2 %all-gather.52.cloned.1.call-done = bf16[1,2048,1024]{1,2,0:T(8,128)(2,1)} async-done(((bf16[1,2048,64]{1,2,0:T(8,128)(2,1)}), bf16[1,2048,1024]{1,2,0:T(8,128)(2,1)}) %all-gather.52.cloned.1.call-update) | async-done | bytes 4194320 | tf_op jit(solution)/shard_map/all_gather | solution.py:38
  268.0 29.5 all-reduce.54.cloned.1.call-done
  299.1 49.9 %all-gather.54.cloned.1.call-done = bf16[1,1024,3,512]{3,1,2,0:T(8,128)(2,1)} async-done(((bf16[1,64,3,512]{3,1,2,0:T(8,128)(2,1)}), bf16[1,1024,3,512]{3,1,2,0:T(8,128)(2,1)}) %all-gather.54.cloned.1.call-update) | async-done | bytes 3145744 | tf_op jit(solution)/shard_map/all_gather | solution.py:32
  392.8 29.4 all-reduce.56.cloned.1.call-done
  423.8 56.5 %all-gather.58.cloned.1.call-done = bf16[1,1024,2048]{2,1,0:T(8,128)(2,1)} async-done(((bf16[1,64,2048]{2,1,0:T(8,128)(2,1)}), bf16[1,1024,2048]{2,1,0:T(8,128)(2,1)}) %all-gather.58.cloned.1.call-update) | async-done | bytes 4194320 | tf_op jit(solution)/shard_map/all_gather | solution.py:37
  487.5 49.5 %all-gather.60.cloned.1.call-done = bf16[1,2048,1024]{1,2,0:T(8,128)(2,1)} async-done(((bf16[1,2048,64]{1,2,0:T(8,128)(2,1)}), bf16[1,2048,1024]{1,2,0:T(8,128)(2,1)}) %all-gather.60.cloned.1.call-update) | async-done | bytes 4194320 | tf_op jit(solution)/shard_map/all_gather | solution.py:38
  543.3 29.7 all-reduce.58.cloned.1.call-done
  574.8 49.1 %all-gather.62.cloned.1.call-done = bf16[1,1024,3,512]{3,1,2,0:T(8,128)(2,1)} async-done(((bf16[1,64,3,512]{3,1,2,0:T(8,128)(2,1)}), bf16[1,1024,3,512]{3,1,2,0:T(8,128)(2,1)}) %all-gather.62.cloned.1.call-update) | async-done | bytes 3145744 | tf_op jit(solution)/shard_map/all_gather | solution.py:32
  700.6 55.1 %all-gather.66.cloned.1.call-done = bf16[1,1024,2048]{2,1,0:T(8,128)(2,1)} async-done(((bf16[1,64,2048]{2,1,0:T(8,128)(2,1)}), bf16[1,1024,2048]{2,1,0:T(8,128)(2,1)}) %all-gather.66.cloned.1.call-update) | async-done | bytes 4194320 | tf_op jit(solution)/shard_map/all_gather | solution.py:37
  763.1 49.1 %all-gather.68.cloned.1.call-done = bf16[1,2048,1024]{1,2,0:T(8,128)(2,1)} async-done(((bf16[1,2048,64]{1,2,0:T(8,128)(2,1)}), bf16[1,2048,1024]{1,2,0:T(8,128)(2,1)}) %all-gather.68.cloned.1.call-update) | async-done | bytes 4194320 | tf_op jit(solution)/shard_map/all_gather | solution.py:38
  823.4 30.5 all-reduce.62.cloned.1.call-done
  920.0 31.2 all-reduce.64.cloned.1.call-done
  965.7 31.5 all-reduce.66.cloned.1.call-done
  1063.9 31.2 all-reduce.68.cloned.1.call-done
  1109.6 31.5 all-reduce.70.cloned.1.call-done
  1209.6 43.1 all-reduce.74.cloned.1.call-done
  1318.0 86.4 %all-reduce.72.cloned.1.call-done = (f32[1024]{0:T(1024)}, f32[1024]{0:T(1024)}, f32[1024]{0:T(1024)}, f32[1024]{0:T(1024)}, f32[1024]{0:T(1024)}, /*index=5*/f3...) async-done(((f32[1024]{0:T(1024)}, f32[1024]{0:T(1024)}, ...) | async-done | bytes 110608
  1424.0 78.5 %reduce-scatter.41.cloned.1.call-done = f32[512,64]{0,1:T(8,128)} async-done(((f32[512,1024]{0,1:T(8,128)}), f32[512,64]{0,1:T(8,128)}) %reduce-scatter.41.cloned.1.call-update) | async-done | bytes 131088 | tf_op jit(solution)/shard_map/reduce_scatter | solution.py:290
  1502.5 99.4 %reduce-scatter.39.cloned.1.call-done = f32[512,64]{0,1:T(8,128)} async-done(((f32[512,1024]{0,1:T(8,128)}), f32[512,64]{0,1:T(8,128)}) %reduce-scatter.39.cloned.1.call-update) | async-done | bytes 131088 | tf_op jit(solution)/shard_map/reduce_scatter | solution.py:290
  1601.9 99.0 %reduce-scatter.37.cloned.1.call-done = f32[512,64]{0,1:T(8,128)} async-done(((f32[512,1024]{0,1:T(8,128)}), f32[512,64]{0,1:T(8,128)}) %reduce-scatter.37.cloned.1.call-update) | async-done | bytes 131088 | tf_op jit(solution)/shard_map/reduce_scatter | solution.py:290
  1702.7 262.1 %reduce-scatter.35.cloned.1.call-done = f32[64,3,512]{2,0,1:T(8,128)} async-done(((f32[1024,3,512]{2,0,1:T(8,128)}), f32[64,3,512]{2,0,1:T(8,128)}) %reduce-scatter.35.cloned.1.call-update) | async-done | bytes 393232 | tf_op jit(solution)/shard_map/reduce_scatter | solution.py:289
  1964.8 264.1 %reduce-scatter.33.cloned.1.call-done = f32[64,3,512]{2,0,1:T(8,128)} async-done(((f32[1024,3,512]{2,0,1:T(8,128)}), f32[64,3,512]{2,0,1:T(8,128)}) %reduce-scatter.33.cloned.1.call-update) | async-done | bytes 393232 | tf_op jit(solution)/shard_map/reduce_scatter | solution.py:289
  2228.9 263.9 %reduce-scatter.31.cloned.1.call-done = f32[64,3,512]{2,0,1:T(8,128)} async-done(((f32[1024,3,512]{2,0,1:T(8,128)}), f32[64,3,512]{2,0,1:T(8,128)}) %reduce-scatter.31.cloned.1.call-update) | async-done | bytes 393232 | tf_op jit(solution)/shard_map/reduce_scatter | solution.py:289
  2495.1 345.5 %reduce-scatter.47.cloned.1.call-done = f32[64,2048]{1,0:T(8,128)} async-done(((f32[1024,2048]{1,0:T(8,128)}), f32[64,2048]{1,0:T(8,128)}) %reduce-scatter.47.cloned.1.call-update) | async-done | bytes 524304 | tf_op jit(solution)/shard_map/reduce_scatter | solution.py:294
  2840.6 348.4 %reduce-scatter.45.cloned.1.call-done = f32[64,2048]{1,0:T(8,128)} async-done(((f32[1024,2048]{1,0:T(8,128)}), f32[64,2048]{1,0:T(8,128)}) %reduce-scatter.45.cloned.1.call-update) | async-done | bytes 524304 | tf_op jit(solution)/shard_map/reduce_scatter | solution.py:294
  3189.0 348.2 %reduce-scatter.43.cloned.1.call-done = f32[64,2048]{1,0:T(8,128)} async-done(((f32[1024,2048]{1,0:T(8,128)}), f32[64,2048]{1,0:T(8,128)}) %reduce-scatter.43.cloned.1.call-update) | async-done | bytes 524304 | tf_op jit(solution)/shard_map/reduce_scatter | solution.py:294
  3539.8 345.7 %reduce-scatter.53.cloned.1.call-done = f32[2048,64]{0,1:T(8,128)} async-done(((f32[2048,1024]{0,1:T(8,128)}), f32[2048,64]{0,1:T(8,128)}) %reduce-scatter.53.cloned.1.call-update) | async-done | bytes 524304 | tf_op jit(solution)/shard_map/reduce_scatter | solution.py:295
  3885.5 348.3 %reduce-scatter.51.cloned.1.call-done = f32[2048,64]{0,1:T(8,128)} async-done(((f32[2048,1024]{0,1:T(8,128)}), f32[2048,64]{0,1:T(8,128)}) %reduce-scatter.51.cloned.1.call-update) | async-done | bytes 524304 | tf_op jit(solution)/shard_map/reduce_scatter | solution.py:295
  4233.9 348.4 %reduce-scatter.49.cloned.1.call-done = f32[2048,64]{0,1:T(8,128)} async-done(((f32[2048,1024]{0,1:T(8,128)}), f32[2048,64]{0,1:T(8,128)}) %reduce-scatter.49.cloned.1.call-update) | async-done | bytes 524304 | tf_op jit(solution)/shard_map/reduce_scatter | solution.py:295
  (776 shorter events, 539.2 us)
Async XLA Ops:
  9.4 102.2 %all-gather.48.cloned.1.call-start = ((), (), s32[]{:S(2)}) async-start(), calls=%async_computation.47 | async-start | bytes 1114112 | tf_op jit(solution)/shard_map/all_gather | solution.py:33
  10.2 136.3 %all-reduce.52.cloned.1.call-start = ((), (), s32[]{:S(2)}) async-start(), calls=%async_computation.18 | async-start | bytes 1310720 | tf_op jit(solution)/shard_map/psum | solution.py:25
  114.4 90.3 %all-gather.50.cloned.1.call-start = ((), (), s32[]{:S(2)}) async-start(), calls=%async_computation.48 | async-start | bytes 4456448 | tf_op jit(solution)/shard_map/all_gather | solution.py:37
  115.3 146.4 %all-gather.52.cloned.1.call-start = ((), (), s32[]{:S(2)}) async-start(), calls=%async_computation.49 | async-start | bytes 4456448 | tf_op jit(solution)/shard_map/all_gather | solution.py:38
  117.4 180.1 %all-reduce.54.cloned.1.call-start = ((), (), s32[]{:S(2)}) async-start(), calls=%async_computation.19 | async-start | bytes 1310720 | tf_op jit(solution)/shard_map/psum | solution.py:25
  266.3 82.7 %all-gather.54.cloned.1.call-start = ((), (), s32[]{:S(2)}) async-start(), calls=%async_computation.50 | async-start | bytes 3342336 | tf_op jit(solution)/shard_map/all_gather | solution.py:32
  267.1 121.1 %all-gather.56.cloned.1.call-start = ((), (), s32[]{:S(2)}) async-start(), calls=%async_computation.51 | async-start | bytes 1114112 | tf_op jit(solution)/shard_map/all_gather | solution.py:33
  267.8 154.4 %all-reduce.56.cloned.1.call-start = ((), (), s32[]{:S(2)}) async-start(), calls=%async_computation.20 | async-start | bytes 1310720 | tf_op jit(solution)/shard_map/psum | solution.py:25
  390.9 89.4 %all-gather.58.cloned.1.call-start = ((), (), s32[]{:S(2)}) async-start(), calls=%async_computation.52 | async-start | bytes 4456448 | tf_op jit(solution)/shard_map/all_gather | solution.py:37
  391.5 145.5 %all-gather.60.cloned.1.call-start = ((), (), s32[]{:S(2)}) async-start(), calls=%async_computation.53 | async-start | bytes 4456448 | tf_op jit(solution)/shard_map/all_gather | solution.py:38
  392.2 180.8 %all-reduce.58.cloned.1.call-start = ((), (), s32[]{:S(2)}) async-start(), calls=%async_computation.21 | async-start | bytes 1310720 | tf_op jit(solution)/shard_map/psum | solution.py:25
  541.8 82.1 %all-gather.62.cloned.1.call-start = ((), (), s32[]{:S(2)}) async-start(), calls=%async_computation.54 | async-start | bytes 3342336 | tf_op jit(solution)/shard_map/all_gather | solution.py:32
  542.6 121.5 %all-gather.64.cloned.1.call-start = ((), (), s32[]{:S(2)}) async-start(), calls=%async_computation.55 | async-start | bytes 1114112 | tf_op jit(solution)/shard_map/all_gather | solution.py:33
  543.1 155.1 %all-reduce.60.cloned.1.call-start = ((), (), s32[]{:S(2)}) async-start(), calls=%async_computation.22 | async-start | bytes 1310720 | tf_op jit(solution)/shard_map/psum | solution.py:25
  666.7 89.0 %all-gather.66.cloned.1.call-start = ((), (), s32[]{:S(2)}) async-start(), calls=%async_computation.56 | async-start | bytes 4456448 | tf_op jit(solution)/shard_map/all_gather | solution.py:37
  667.3 144.9 %all-gather.68.cloned.1.call-start = ((), (), s32[]{:S(2)}) async-start(), calls=%async_computation.57 | async-start | bytes 4456448 | tf_op jit(solution)/shard_map/all_gather | solution.py:38
  667.9 186.1 %all-reduce.62.cloned.1.call-start = ((), (), s32[]{:S(2)}) async-start(), calls=%async_computation.23 | async-start | bytes 1310720 | tf_op jit(solution)/shard_map/psum | solution.py:25
  872.9 78.3 %all-reduce.64.cloned.1.call-start = ((), (), s32[]{:S(2)}) async-start(), calls=%async_computation.26 | async-start | bytes 1310720 | tf_op jit(solution)/shard_map/psum | solution.py:25
  1156.7 96.0 %all-reduce.74.cloned.1.call-start = ((), (), s32[]{:S(2)}) async-start(), calls=%async_computation.59 | async-start | bytes 2621440 | tf_op jit(solution)/shard_map/psum | solution.py:25
  1207.0 197.4 %all-reduce.72.cloned.1.call-start = ((), (), s32[]{:S(2)}) async-start(), calls=%async_computation.58 | async-start | bytes 221184
  1255.8 246.7 %reduce-scatter.41.cloned.1.call-start = ((), (), s32[]{:S(2)}) async-start(), calls=%async_computation.39 | async-start | bytes 2228224 | tf_op jit(solution)/shard_map/reduce_scatter | solution.py:290
  1258.8 343.1 %reduce-scatter.39.cloned.1.call-start = ((), (), s32[]{:S(2)}) async-start(), calls=%async_computation.38 | async-start | bytes 2228224 | tf_op jit(solution)/shard_map/reduce_scatter | solution.py:290
  1261.7 439.2 %reduce-scatter.37.cloned.1.call-start = ((), (), s32[]{:S(2)}) async-start(), calls=%async_computation.37 | async-start | bytes 2228224 | tf_op jit(solution)/shard_map/reduce_scatter | solution.py:290
  1264.7 700.2 %reduce-scatter.35.cloned.1.call-start = ((), (), s32[]{:S(2)}) async-start(), calls=%async_computation.36 | async-start | bytes 6684672 | tf_op jit(solution)/shard_map/reduce_scatter | solution.py:289
  1269.5 959.4 %reduce-scatter.33.cloned.1.call-start = ((), (), s32[]{:S(2)}) async-start(), calls=%async_computation.35 | async-start | bytes 6684672 | tf_op jit(solution)/shard_map/reduce_scatter | solution.py:289
  1274.4 1218.4 %reduce-scatter.31.cloned.1.call-start = ((), (), s32[]{:S(2)}) async-start(), calls=%async_computation.34 | async-start | bytes 6684672 | tf_op jit(solution)/shard_map/reduce_scatter | solution.py:289
  1279.3 1561.4 %reduce-scatter.47.cloned.1.call-start = ((), (), s32[]{:S(2)}) async-start(), calls=%async_computation.42 | async-start | bytes 8912896 | tf_op jit(solution)/shard_map/reduce_scatter | solution.py:294
  1285.3 1903.7 %reduce-scatter.45.cloned.1.call-start = ((), (), s32[]{:S(2)}) async-start(), calls=%async_computation.41 | async-start | bytes 8912896 | tf_op jit(solution)/shard_map/reduce_scatter | solution.py:294
  1291.3 2245.9 %reduce-scatter.43.cloned.1.call-start = ((), (), s32[]{:S(2)}) async-start(), calls=%async_computation.40 | async-start | bytes 8912896 | tf_op jit(solution)/shard_map/reduce_scatter | solution.py:294
  1297.2 2588.4 %reduce-scatter.53.cloned.1.call-start = ((), (), s32[]{:S(2)}) async-start(), calls=%async_computation.45 | async-start | bytes 8912896 | tf_op jit(solution)/shard_map/reduce_scatter | solution.py:295
  1303.1 2930.8 %reduce-scatter.51.cloned.1.call-start = ((), (), s32[]{:S(2)}) async-start(), calls=%async_computation.44 | async-start | bytes 8912896 | tf_op jit(solution)/shard_map/reduce_scatter | solution.py:295
  1309.1 3273.1 %reduce-scatter.49.cloned.1.call-start = ((), (), s32[]{:S(2)}) async-start(), calls=%async_computation.43 | async-start | bytes 8912896 | tf_op jit(solution)/shard_map/reduce_scatter | solution.py:295
  (214 other events, 3953.1 us)
Sparse Core Ops, SparseCore 0:
  11.0 53.3 all-gather.45
  67.3 41.8 all-gather.47
  114.5 32.0 all-reduce.51
  149.6 55.0 all-gather.49
  207.6 54.0 all-gather.51
  300.4 48.5 all-gather.53
  351.3 36.8 all-gather.55
  425.2 55.0 all-gather.57
  482.9 54.0 all-gather.59
  575.4 48.5 all-gather.61
  626.1 37.7 all-gather.63
  666.8 31.3 all-reduce.59
  700.6 55.0 all-gather.65
  758.1 54.0 all-gather.67
  822.9 31.0 all-reduce.61
  965.2 32.0 all-reduce.65
  1064.0 31.0 all-reduce.67
  1109.0 32.0 all-reduce.69
  1207.1 45.5 all-reduce.73
  1258.6 145.7 all-reduce.71
  1406.6 95.8 reduce-scatter.40
  1504.8 97.0 reduce-scatter.38
  1604.0 96.8 reduce-scatter.36
  1703.2 261.5 reduce-scatter.34
  1967.1 261.7 reduce-scatter.32
  2231.0 261.6 reduce-scatter.30
  2494.9 345.6 reduce-scatter.46
  2842.9 346.0 reduce-scatter.44
  3191.1 346.0 reduce-scatter.42
  3539.5 346.0 reduce-scatter.52
  3887.8 346.0 reduce-scatter.50
  4236.2 346.0 reduce-scatter.48
  (10 shorter events, 264.2 us)
where the time goes:
time: 4600 us; the launch traced here: 4590 us
  waiting for transfers between devices  4120 us (90%)
  matrix products  169 us (4%)
  blocking collectives  137 us (3%)
  local copies, waits for them, and re-layouts  84.3 us (2%)
  other arithmetic  63 us (1%)
    reduce_scatter x3, waiting for transfers between devices, body(): lax.psum_scatter(layer_grads[8], ('fsdp', 'ctx'), scatter_dimension=1, ti...  1040 us
    reduce_scatter x3, waiting for transfers between devices, body(): lax.psum_scatter(layer_grads[7], ('fsdp', 'ctx'), scatter_dimension=0, ti...  1040 us
    reduce_scatter x3, waiting for transfers between devices, body(): lax.psum_scatter(layer_grads[2], ('fsdp', 'ctx'), scatter_dimension=0, ti...  790 us
    psum x11, waiting for transfers between devices, head_sum(): return lax.psum(partial_rows, 'tp')  344 us
    reduce_scatter x3, waiting for transfers between devices, body(): lax.psum_scatter(layer_grads[3], ('fsdp', 'ctx'), scatter_dimension=1, ti...  277 us
    all_gather x3, waiting for transfers between devices, fetch_weights(): lax.all_gather(up_w, ('fsdp', 'ctx'), axis=0, tiled=True)  168 us
    all_gather x3, waiting for transfers between devices, fetch_weights(): lax.all_gather(down_w, ('fsdp', 'ctx'), axis=1, tiled=True)  149 us
    all_gather x3, waiting for transfers between devices, fetch_weights(): lax.all_gather(qkv_w, ('fsdp', 'ctx'), axis=0, tiled=True)  99 us
  transfers between devices with their start and end apart: 42, of which 39 were waited for; matrix products, arithmetic and copies ran while one was open for 4% of the time, Pallas kernels for 0%

commit v1 on v0

v1 whole, which is shorter than its diff:
```python
import functools

import jax
import jax.numpy as jnp
from jax import lax
from jax.experimental import pallas as pl
from jax.experimental.pallas import tpu as pltpu
from jax.sharding import PartitionSpec as P

HEAD_DIM = 64
EPS = 1e-05
NEG = -30000.0
MESH = pl.DeviceIdType.MESH
PARTS = 6
BF16 = jnp.bfloat16
F32 = jnp.float32


def flip(index, bit):
    size = 2**bit
    return index + size - 2 * size * ((index // size) % 2)


def flip_all(index, bits):
    for bit in bits:
        index = flip(index, bit)
    return index


def subsets(bits):
    found = [()]
    for bit in bits:
        found = found + [entry + (bit,) for entry in found]
    return found


def orders(fsdp_size):
    top = fsdp_size.bit_length() - 1
    bits = list(range(1, top))
    half = len(bits) // 2
    return bits, bits[half:] + bits[:half]


class Link:
    def __init__(self, send_sem, recv_sem):
        self.send_sem, self.recv_sem, self.used, self.sent = send_sem, recv_sem, 0, []

    def push(self, src, dst, device):
        at = self.used
        self.used += 1
        copy = pltpu.make_async_remote_copy(
            src_ref=src,
            dst_ref=dst,
            send_sem=self.send_sem.at[at],
            recv_sem=self.recv_sem.at[at],
            device_id=device,
            device_id_type=MESH,
        )
        copy.start()
        self.sent.append(copy)
        return copy

    def drain(self):
        for copy in self.sent:
            copy.wait_send()
        self.sent = []


def greet(fsdp_size, ctx_size, with_tp):
    me, ctx, tp = lax.axis_index("fsdp"), lax.axis_index("ctx"), lax.axis_index("tp")
    barrier = pltpu.get_barrier_semaphore()
    count = 0
    for bit in range(fsdp_size.bit_length() - 1):
        pl.semaphore_signal(
            barrier, inc=1, device_id={"fsdp": flip(me, bit)}, device_id_type=MESH
        )
        count += 1
    if ctx_size > 1:
        pl.semaphore_signal(barrier, inc=1, device_id={"ctx": 1 - ctx}, device_id_type=MESH)
        count += 1
    if with_tp:
        pl.semaphore_signal(barrier, inc=1, device_id={"tp": 1 - tp}, device_id_type=MESH)
        count += 1
    pl.semaphore_wait(barrier, count)


def rows_of(start, rows):
    return pl.ds(pl.multiple_of(start * rows, rows), rows)


def gather_pushes(fsdp_size, ctx_size):
    steps = fsdp_size.bit_length() - 2
    return (ctx_size - 1) + ctx_size * (2**steps - 1) + 2**steps


class Gather:
    def __init__(self, link, ctx_size, own, whole, block, order, local_sem):
        self.link, self.own, self.whole, self.block, self.order = link, own, whole, block, order
        self.ctx_size = ctx_size
        self.me, self.ctx = lax.axis_index("fsdp"), lax.axis_index("ctx")
        self.waits = {}
        self.stay = pltpu.make_async_copy(own, self.rows(self.me, self.ctx), local_sem)

    def rows(self, fsdp, ctx):
        return self.whole.at[rows_of(fsdp * self.ctx_size + ctx, self.block)]

    def spread(self, stream, step):
        ctx = self.ctx if stream == 0 else 1 - self.ctx
        bit = self.order[step]
        to = {"fsdp": flip(self.me, bit)}
        copies = []
        for entry in subsets(self.order[:step]):
            place = self.rows(flip_all(self.me, entry), ctx)
            source = self.own if (stream == 0 and not entry) else place
            copies.append(self.link.push(source, place, to))
        self.waits[stream, step] = copies

    def arrive(self, *key):
        for copy in self.waits.pop(key):
            copy.wait_recv()

    def start(self):
        self.stay.start()
        if self.ctx_size > 1:
            self.waits["ctx",] = [
                self.link.push(self.own, self.rows(self.me, self.ctx), {"ctx": 1 - self.ctx})
            ]
        self.spread(0, 0)

    def next_step(self, stream, step):
        self.arrive(stream, step - 1)
        self.spread(stream, step)

    def other(self):
        self.arrive("ctx")
        self.spread(1, 0)

    def core(self):
        last = len(self.order) - 1
        for stream in range(self.ctx_size):
            self.arrive(stream, last)
        self.stay.wait()
        both = self.block * self.ctx_size
        copies = []
        for entry in subsets(self.order):
            place = self.whole.at[rows_of(flip_all(self.me, entry), both)]
            copies.append(self.link.push(place, place, {"fsdp": flip(self.me, 0)}))
        self.waits["core",] = copies

    def finish(self):
        self.arrive("core")

    def events(self):
        found = [self.start]
        for step in range(1, len(self.order)):
            found.append(functools.partial(self.next_step, 0, step))
        if self.ctx_size > 1:
            found.append(self.other)
            for step in range(1, len(self.order)):
                found.append(functools.partial(self.next_step, 1, step))
        return found + [self.core, self.finish]


def skewed(groups, skew):
    timed = []
    for at, events in enumerate(groups):
        for place, event in enumerate(events):
            timed.append((0 if place == 0 else place + at * skew, at, place, event))
    return [entry[3] for entry in sorted(timed, key=lambda entry: entry[:3])]


def in_step(first, second):
    def run(one, two):
        one()
        two()

    return [functools.partial(run, one, two) for one, two in zip(first, second)]


def gather_kernel(ctx_size, fsdp_size, with_small, *refs):
    if with_small:
        own_ref, small_ref, whole_ref, small_whole, send_sem, recv_sem, local_sem = refs
    else:
        own_ref, whole_ref, send_sem, recv_sem, local_sem = refs
    greet(fsdp_size, ctx_size, False)
    link = Link(send_sem, recv_sem)
    both = orders(fsdp_size)
    groups = []
    if with_small:
        groups.append(
            Gather(
                link, ctx_size, small_ref, small_whole, small_ref.shape[0], both[0], local_sem.at[PARTS]
            ).events()
        )
    for pair in range(PARTS // 2):
        groups.append(
            in_step(
                *[
                    Gather(
                        link,
                        ctx_size,
                        own_ref.at[part],
                        whole_ref.at[part],
                        own_ref.shape[1],
                        both[part % 2],
                        local_sem.at[part],
                    ).events()
                    for part in (2 * pair, 2 * pair + 1)
                ]
            )
        )
    for event in skewed(groups, 1):
        event()
    link.drain()


def gather_layer(mesh, own, small=None):
    fsdp_size, ctx_size = mesh.shape["fsdp"], mesh.shape["ctx"]
    parts, block, columns = own.shape
    everyone = fsdp_size * ctx_size
    out_shape = [jax.ShapeDtypeStruct((parts, everyone * block, columns), own.dtype)]
    operands = [own]
    if small is not None:
        operands.append(small)
        out_shape.append(jax.ShapeDtypeStruct((everyone * small.shape[0], small.shape[1]), small.dtype))
    pushes = gather_pushes(fsdp_size, ctx_size) * (parts + len(operands) - 1)
    any_space = pl.BlockSpec(memory_space=pl.ANY)
    return pl.pallas_call(
        functools.partial(gather_kernel, ctx_size, fsdp_size, small is not None),
        out_shape=out_shape,
        in_specs=[any_space] * len(operands),
        out_specs=[any_space] * len(out_shape),
        scratch_shapes=[
            pltpu.SemaphoreType.DMA((pushes,)),
            pltpu.SemaphoreType.DMA((pushes,)),
            pltpu.SemaphoreType.DMA((parts + 1,)),
        ],
        compiler_params=pltpu.CompilerParams(
            collective_id=0 if small is None else 1, has_side_effects=True
        ),
        name="gather_layer",
    )(*operands)


class Scatter:
    def __init__(self, link, ctx_size, terms, held, arrived, last, order, load_sem, write):
        self.link, self.terms, self.held, self.arrived, self.last = link, terms, held, arrived, last
        self.ctx_size, self.order, self.load_sem, self.write = ctx_size, order, load_sem, write
        self.me, self.ctx = lax.axis_index("fsdp"), lax.axis_index("ctx")
        self.both = held.shape[1]
        self.slots = held.shape[0]
        self.flips = []
        for slot in range(self.slots):
            chosen = [
                bit for at, bit in enumerate(order) if (slot >> (len(order) - 1 - at)) % 2 == 1
            ]
            self.flips.append(chosen)
        self.base = 0

    def start(self):
        other = flip(self.me, 0)
        self.copies, self.loads = [], []
        for slot, chosen in enumerate(self.flips):
            theirs = self.terms.at[rows_of(flip_all(other, chosen), self.both)]
            ours = self.terms.at[rows_of(flip_all(self.me, chosen), self.both)]
            self.copies.append(self.link.push(theirs, self.arrived.at[slot], {"fsdp": other}))
            load = pltpu.make_async_copy(ours, self.held.at[slot], self.load_sem.at[slot])
            load.start()
            self.loads.append(load)

    def take(self, count, base):
        for copy in self.copies:
            copy.wait_recv()
        for slot in range(count):
            self.held[slot] = self.held[slot] + self.arrived[base + slot]

    def step(self, at):
        count = self.slots >> at
        if at == 0:
            for load in self.loads:
                load.wait()
        self.take(count, self.base)
        self.base += count
        half = count // 2
        self.copies = [
            self.link.push(
                self.held.at[pl.ds(half, half)],
                self.arrived.at[pl.ds(self.base, half)],
                {"fsdp": flip(self.me, self.order[at])},
            )
        ]

    def across(self):
        self.take(1, self.base)
        if self.ctx_size > 1:
            block = self.both // self.ctx_size
            self.copies = [
                self.link.push(
                    self.held.at[0, rows_of(1 - self.ctx, block)],
                    self.last,
                    {"ctx": 1 - self.ctx},
                )
            ]

    def finish(self):
        block = self.both // self.ctx_size
        total = self.held[0, rows_of(self.ctx, block)].astype(F32)
        if self.ctx_size > 1:
            for copy in self.copies:
                copy.wait_recv()
            total = total + self.last[...].astype(F32)
        self.write(total)

    def events(self):
        found = [self.start]
        for at in range(len(self.order)):
            found.append(functools.partial(self.step, at))
        return found + [self.across, self.finish]


class Total:
    def __init__(self, link, fsdp_size, ctx_size, held, arrived):
        self.link, self.held, self.arrived = link, held, arrived
        me, ctx = lax.axis_index("fsdp"), lax.axis_index("ctx")
        self.partners = [{"fsdp": flip(me, bit)} for bit in range(fsdp_size.bit_length() - 1)]
        if ctx_size > 1:
            self.partners.append({"ctx": 1 - ctx})

    def step(self, at):
        if at > 0:
            self.copy.wait_recv()
            self.held[at] = self.held[at - 1] + self.arrived[at - 1]
        if at < len(self.partners):
            self.copy = self.link.push(self.held.at[at], self.arrived.at[at], self.partners[at])

    def events(self):
        return [functools.partial(self.step, at) for at in range(len(self.partners) + 1)]


def scatter_pushes(fsdp_size):
    steps = fsdp_size.bit_length() - 2
    return 2**steps + steps + 1


def scatter_kernel(
    ctx_size,
    fsdp_size,
    terms_ref,
    small_ref,
    out_ref,
    small_out,
    held,
    arrived,
    last,
    small_held,
    small_arrived,
    send_sem,
    recv_sem,
    load_sem,
):
    small_held[0] = small_ref[...]
    greet(fsdp_size, ctx_size, False)
    link = Link(send_sem, recv_sem)
    both = [order[::-1] for order in orders(fsdp_size)]
    total = Total(link, fsdp_size, ctx_size, small_held, small_arrived)
    groups = [total.events()]

    def writer(part):
        def write(value):
            out_ref[part] = value

        return write

    for pair in range(PARTS // 2):
        groups.append(
            in_step(
                *[
                    Scatter(
                        link,
                        ctx_size,
                        terms_ref.at[part],
                        held.at[part],
                        arrived.at[part],
                        last.at[part],
                        both[part % 2],
                        load_sem.at[part],
                        writer(part),
                    ).events()
                    for part in (2 * pair, 2 * pair + 1)
                ]
            )
        )
    for event in skewed(groups, 1):
        event()
    small_out[...] = small_held[len(total.partners)]
    link.drain()


def scatter_layer(mesh, terms, small):
    fsdp_size, ctx_size = mesh.shape["fsdp"], mesh.shape["ctx"]
    parts, depth, columns = terms.shape
    both = depth // fsdp_size
    block = both // ctx_size
    slots = fsdp_size // 2
    steps = fsdp_size.bit_length() - 1 + (ctx_size > 1)
    pushes = scatter_pushes(fsdp_size) * parts + steps
    vmem = pl.BlockSpec(memory_space=pltpu.VMEM)
    return pl.pallas_call(
        functools.partial(scatter_kernel, ctx_size, fsdp_size),
        out_shape=[
            jax.ShapeDtypeStruct((parts, block, columns), F32),
            jax.ShapeDtypeStruct(small.shape, F32),
        ],
        in_specs=[pl.BlockSpec(memory_space=pl.ANY), vmem],
        out_specs=[vmem, vmem],
        scratch_shapes=[
            pltpu.VMEM((parts, slots, both, columns), BF16),
            pltpu.VMEM((parts, 2 * slots - 1, both, columns), BF16),
            pltpu.VMEM((parts, block, columns), BF16),
            pltpu.VMEM((steps + 1,) + small.shape, F32),
            pltpu.VMEM((steps,) + small.shape, F32),
            pltpu.SemaphoreType.DMA((pushes,)),
            pltpu.SemaphoreType.DMA((pushes,)),
            pltpu.SemaphoreType.DMA((parts, slots)),
        ],
        compiler_params=pltpu.CompilerParams(
            collective_id=2, has_side_effects=True, vmem_limit_bytes=48 * 2**20
        ),
        name="scatter_layer",
    )(terms, small)


def layer_norm(values, norm_gain, norm_shift):
    row_mean = jnp.mean(values, axis=-1, keepdims=True)
    centered = values - row_mean
    row_var = jnp.mean(centered * centered, axis=-1, keepdims=True)
    return centered * lax.rsqrt(row_var + EPS) * norm_gain + norm_shift


def gelu_exact(values):
    return jax.nn.gelu(values, approximate=False)


def head_sum(partial_rows):
    return lax.psum(partial_rows, "tp")


def dot(spec, left, right):
    return jnp.einsum(spec, left, right, preferred_element_type=F32)


def masked_scores(query_heads, key_heads, key_live, score_scale):
    raw_scores = dot("nqhd,nkhd->nhqk", query_heads, key_heads) * score_scale
    return jnp.where(key_live, raw_scores, NEG)


def body(
    mesh,
    tokens,
    lengths,
    cotangent,
    attn_gain,
    attn_shift,
    qkv_weight,
    qv_bias,
    out_weight,
    out_bias,
    mlp_gain,
    mlp_shift,
    up_weight,
    up_bias,
    down_weight,
    down_bias,
):
    images, local_slots, width = tokens.shape
    fsdp_size, ctx_size = mesh.shape["fsdp"], mesh.shape["ctx"]
    everyone = fsdp_size * ctx_size
    slots_all = local_slots * ctx_size
    layers, block, _, cols = qkv_weight.shape
    heads_here = cols // HEAD_DIM
    units = up_weight.shape[2]
    score_scale = HEAD_DIM ** (-0.5)
    slot_ids = lax.axis_index("ctx") * local_slots + jnp.arange(local_slots, dtype=jnp.int32)
    row_mask = (slot_ids[None, :] < lengths[:, None]).astype(F32)[:, :, None]
    key_live = (jnp.arange(slots_all, dtype=jnp.int32)[None, :] < lengths[:, None])[
        :, None, None, :
    ]
    vectors = jnp.stack((attn_gain, attn_shift, out_bias, mlp_gain, mlp_shift, down_bias), axis=1)
    flat = vectors.reshape(-1)
    small_rows = 16 * -(-flat.size // (16 * 2 * cols))
    small = jnp.pad(flat, (0, small_rows * 2 * cols - flat.size)).reshape(small_rows, 2 * cols)
    out_t = jnp.swapaxes(out_weight, 1, 2)
    down_t = jnp.swapaxes(down_weight, 1, 2)

    def own_parts(at):
        return jnp.stack(
            (
                qkv_weight[at, :, 0:2].reshape(block, 2 * cols),
                jnp.concatenate((qkv_weight[at, :, 2], out_t[at]), axis=1),
                up_weight[at, :, : units // 2],
                up_weight[at, :, units // 2 :],
                down_t[at, :, : units // 2],
                down_t[at, :, units // 2 :],
            )
        )

    weights = []
    for at in range(layers):
        if at == 0:
            whole, small_whole = gather_layer(mesh, own_parts(at), small)
        else:
            (whole,) = gather_layer(mesh, own_parts(at))
        weights.append(whole)
    gathered = small_whole.reshape(everyone, small_rows * 2 * cols)[:, : flat.size]
    vectors = jnp.swapaxes(gathered.reshape(everyone, layers * 6, block), 0, 1)
    vectors = vectors.reshape(layers, 6, width).astype(F32)

    stream = tokens.astype(F32) * row_mask
    kept = []
    for at in range(layers):
        whole = weights[at]
        gain_a, shift_a, out_b, gain_b, shift_b, down_b = [vectors[at, i] for i in range(6)]
        bias_qv = qv_bias[at].astype(F32)
        normed_a = layer_norm(stream, gain_a, shift_a).astype(BF16)
        queries = (dot("nsd,df->nsf", normed_a, whole[0, :, :cols]) + bias_qv[0]).astype(BF16)
        keys_own = dot("nsd,df->nsf", normed_a, whole[0, :, cols:]).astype(BF16)
        values_own = (dot("nsd,df->nsf", normed_a, whole[1, :, :cols]) + bias_qv[1]).astype(BF16)
        both = lax.all_gather(jnp.concatenate((keys_own, values_own), -1), "ctx", axis=1, tiled=True)
        query_heads = queries.reshape(images, local_slots, heads_here, HEAD_DIM)
        key_heads = both[:, :, :cols].reshape(images, slots_all, heads_here, HEAD_DIM)
        value_heads = both[:, :, cols:].reshape(images, slots_all, heads_here, HEAD_DIM)
        scores = masked_scores(query_heads, key_heads, key_live, score_scale)
        row_top = jnp.max(scores, axis=-1, keepdims=True)
        exp_scores = jnp.exp(scores - row_top)
        row_total = jnp.sum(exp_scores, axis=-1, keepdims=True)
        attn_probs = (exp_scores / row_total).astype(BF16)
        log_total = row_top + jnp.log(row_total)
        attended = dot("nhqk,nkhd->nqhd", attn_probs, value_heads)
        attended = attended.reshape(images, local_slots, cols).astype(BF16)
        branch_a = head_sum(dot("nsf,df->nsd", attended, whole[1, :, cols:]))
        mid = stream + row_mask * (branch_a + out_b)
        normed_b = layer_norm(mid, gain_b, shift_b).astype(BF16)
        hidden_pre = jnp.concatenate(
            [dot("nsd,df->nsf", normed_b, whole[part]) for part in (2, 3)], axis=-1
        ) + up_bias[at].astype(F32)
        hidden = gelu_exact(hidden_pre).astype(BF16)
        halves = (hidden[:, :, : units // 2], hidden[:, :, units // 2 :])
        branch_b = head_sum(
            dot("nsf,df->nsd", halves[0], whole[4]) + dot("nsf,df->nsd", halves[1], whole[5])
        )
        kept.append(
            (
                stream,
                normed_a,
                query_heads,
                key_heads,
                value_heads,
                log_total,
                attended,
                mid,
                normed_b,
                hidden_pre,
                halves,
            )
        )
        stream = mid + row_mask * (branch_b + down_b)
    output = stream.astype(BF16)
    grad_stream = cotangent.astype(F32)
    big, little = [None] * layers, [None] * layers
    for at in reversed(range(layers)):
        (
            layer_in,
            normed_a,
            query_heads,
            key_heads,
            value_heads,
            log_total,
            attended,
            mid,
            normed_b,
            hidden_pre,
            halves,
        ) = kept[at]
        whole = weights[at]
        gain_a, shift_a, out_b, gain_b, shift_b, down_b = [vectors[at, i] for i in range(6)]
        grad_branch_b = row_mask * grad_stream
        grad_down_b = jnp.sum(grad_branch_b, axis=(0, 1))
        low_b = grad_branch_b.astype(BF16)
        grad_down = [dot("nsd,nsf->df", low_b, half) for half in halves]
        grad_hidden = jnp.concatenate(
            [dot("nsd,df->nsf", low_b, whole[part]) for part in (4, 5)], axis=-1
        )
        grad_pre = jax.vjp(gelu_exact, hidden_pre)[1](grad_hidden)[0]
        grad_up_b = jnp.sum(grad_pre, axis=(0, 1))
        low_pre = grad_pre.astype(BF16)
        pre_halves = (low_pre[:, :, : units // 2], low_pre[:, :, units // 2 :])
        grad_up = [dot("nsd,nsf->df", normed_b, half) for half in pre_halves]
        grad_normed_b = head_sum(
            dot("nsf,df->nsd", pre_halves[0], whole[2])
            + dot("nsf,df->nsd", pre_halves[1], whole[3])
        )
        grad_mid_norm, grad_gain_b, grad_shift_b = jax.vjp(layer_norm, mid, gain_b, shift_b)[1](
            grad_normed_b
        )
        grad_mid = grad_stream + grad_mid_norm
        grad_branch_a = row_mask * grad_mid
        grad_out_b = jnp.sum(grad_branch_a, axis=(0, 1))
        low_a = grad_branch_a.astype(BF16)
        grad_out = dot("nsd,nsf->df", low_a, attended)
        grad_att = dot("nsd,df->nsf", low_a, whole[1, :, cols:]).astype(BF16)
        grad_att = grad_att.reshape(images, local_slots, heads_here, HEAD_DIM)
        scores = masked_scores(query_heads, key_heads, key_live, score_scale)
        attn_p = jnp.exp(scores - log_total)
        grad_probs = dot("nqhd,nkhd->nhqk", grad_att, value_heads)
        row_dot = jnp.sum(attn_p * grad_probs, axis=-1, keepdims=True)
        grad_scores = (attn_p * (grad_probs - row_dot)).astype(BF16)
        grad_q = (dot("nhqk,nkhd->nqhd", grad_scores, key_heads) * score_scale).astype(BF16)
        grad_q = grad_q.reshape(images, local_slots, cols)
        grad_k = dot("nhqk,nqhd->nkhd", grad_scores, query_heads) * score_scale
        grad_v = dot("nhqk,nqhd->nkhd", attn_p.astype(BF16), grad_att)
        grad_kv = jnp.concatenate(
            (
                grad_k.reshape(images, slots_all, cols),
                grad_v.reshape(images, slots_all, cols),
            ),
            axis=-1,
        )
        grad_kv = lax.psum_scatter(grad_kv, "ctx", scatter_dimension=1, tiled=True).astype(BF16)
        grad_v = grad_kv[:, :, cols:]
        grad_qv_b = jnp.concatenate(
            (jnp.sum(grad_q.astype(F32), axis=(0, 1)), jnp.sum(grad_v.astype(F32), axis=(0, 1)))
        )
        grad_qk = jnp.concatenate((grad_q, grad_kv[:, :, :cols]), axis=-1)
        terms = [
            dot("nsd,nsf->df", normed_a, grad_qk),
            jnp.concatenate((dot("nsd,nsf->df", normed_a, grad_v), grad_out), axis=1),
            *grad_up,
            *grad_down,
        ]
        grad_normed_a = head_sum(
            dot("nsf,df->nsd", grad_qk, whole[0]) + dot("nsf,df->nsd", grad_v, whole[1, :, :cols])
        )
        grad_in_norm, grad_gain_a, grad_shift_a = jax.vjp(layer_norm, layer_in, gain_a, shift_a)[1](
            grad_normed_a
        )
        grad_stream = grad_mid + grad_in_norm
        rows = [grad_gain_a, grad_shift_a, grad_out_b, grad_gain_b, grad_shift_b, grad_down_b]
        rows.append(grad_qv_b)
        rows.extend(jnp.split(grad_up_b, units // width))
        rows = jnp.pad(jnp.stack(rows), ((0, -len(rows) % 8), (0, 0)))
        big[at], little[at] = scatter_layer(
            mesh, jnp.stack([term.astype(BF16) for term in terms]), rows
        )
    input_grad = grad_stream * row_mask
    big, little = jnp.stack(big), jnp.stack(little)
    here = (lax.axis_index("fsdp") * ctx_size + lax.axis_index("ctx")) * block
    own_vectors = lax.dynamic_slice_in_dim(little[:, :6], here, block, axis=2)
    grad_qkv = jnp.concatenate((big[:, 0], big[:, 1, :, :cols]), axis=2)
    return (
        output,
        input_grad,
        own_vectors[:, 0],
        own_vectors[:, 1],
        grad_qkv.reshape(layers, block, 3, cols),
        little[:, 6].reshape(layers, 2, cols),
        jnp.swapaxes(big[:, 1, :, cols:], 1, 2),
        own_vectors[:, 2],
        own_vectors[:, 3],
        own_vectors[:, 4],
        jnp.concatenate((big[:, 2], big[:, 3]), axis=2),
        little[:, 7 : 7 + units // width].reshape(layers, units),
        jnp.swapaxes(jnp.concatenate((big[:, 4], big[:, 5]), axis=2), 1, 2),
        own_vectors[:, 5],
    )


def solution(mesh):
    place = P(None, ("fsdp", "ctx"))
    rows = P("fsdp", "ctx", None)
    return jax.shard_map(
        functools.partial(body, mesh),
        mesh=mesh,
        in_specs=(
            rows,
            P("fsdp"),
            rows,
            place,
            place,
            P(None, ("fsdp", "ctx"), None, "tp"),
            P(None, None, "tp"),
            P(None, "tp", ("fsdp", "ctx")),
            place,
            place,
            place,
            P(None, ("fsdp", "ctx"), "tp"),
            P(None, "tp"),
            P(None, "tp", ("fsdp", "ctx")),
            place,
        ),
        out_specs=(
            rows,
            rows,
            place,
            place,
            P(None, ("fsdp", "ctx"), None, "tp"),
            P(None, None, "tp"),
            P(None, "tp", ("fsdp", "ctx")),
            place,
            place,
            place,
            P(None, ("fsdp", "ctx"), "tp"),
            P(None, "tp"),
            P(None, "tp", ("fsdp", "ctx")),
            place,
        ),
        check_vma=False,
    )
```

time: 4600 us -> 2480 us (0.54)
  waiting for transfers between devices: 4120 us -> 242 us
  blocking collectives: 137 us -> 1450 us
  Pallas kernels: 0 us -> 433 us
    reduce_scatter x18 -> x0, waiting for transfers between devices: 3260 us -> none  [the longest x3 1040 us: body(): lax.psum_scatter(layer_grads[8], ('fsdp', 'ctx'), scatter_dimension=1, ti...]
    unnamed x1 -> x3, blocking collectives: 64.4 us -> 1400 us
    pallas_call x0 -> x6, Pallas kernels: none -> 433 us  [the longest x3 227 us: scatter_layer(): pl.pallas_call(functools.partial(scatter_kernel, ctx_size, fsdp_size), ou...]
    all_gather x12 -> x0, waiting for transfers between devices: 418 us -> none  [the longest x3 168 us: fetch_weights(): lax.all_gather(up_w, ('fsdp', 'ctx'), axis=0, tiled=True)]
    psum x11, waiting for transfers between devices: 344 us -> 241 us  [head_sum(): return lax.psum(partial_rows, 'tp')]
    unnamed x43 -> x11, waiting for transfers between devices: 91.8 us -> 0.18 us
    dot_general x54 -> x84, matrix products: 169 us -> 182 us  [dot(): return jnp.einsum(spec, left, right, preferred_element_type=F32)]
  transfers between devices with their start and end apart: 42 -> 11, of which waited for: 39 -> 9; matrix products, arithmetic and copies ran while one was open for 4% -> 2% of each run, Pallas kernels for 0% -> 5%
where the time goes in v1:
time: 2480 us; the launch traced here: 2470 us
  blocking collectives  1450 us (58%)
  Pallas kernels  433 us (17%)
  waiting for transfers between devices  242 us (10%)
  matrix products  182 us (7%)
  other arithmetic  82.2 us (3%)
  local copies, waits for them, and re-layouts  60.3 us (2%)
    unnamed x3, blocking collectives  1400 us
    psum x11, waiting for transfers between devices, head_sum(): return lax.psum(partial_rows, 'tp')  241 us
    pallas_call x3, Pallas kernels, scatter_layer(): pl.pallas_call(functools.partial(scatter_kernel, ctx_size, fsdp_size), ou...  227 us
    pallas_call x3, Pallas kernels, gather_layer(): pl.pallas_call(functools.partial(gather_kernel, ctx_size, fsdp_size, smal...  206 us
    dot_general x84, matrix products, dot(): return jnp.einsum(spec, left, right, preferred_element_type=F32)  182 us
  transfers between devices with their start and end apart: 11, of which 9 were waited for; matrix products, arithmetic and copies ran while one was open for 2% of the time, Pallas kernels for 5%

profile of v1, /device:TPU:0, one launch (start us, length us, event | category | flops | bytes accessed | tf_op | source)
XLA Modules:
  0.0 2467.2 jit_solution(4138492039611669111)
XLA Ops:
  15.1 74.8 %gather_layer.3 = (bf16[6,1024,1024]{2,1,0:T(8,128)(2,1)}, bf16[256,1024]{1,0:T(8,128)(2,1)}) custom-call(bf16[6,64,1024]{2,1,0:T(8,128)(2,1)} %copy-done.83, bf16[16,1024]{1,0:T(8,128)(2,1)} %reshape.2686.refs_1_), custom_call_target="tpu_custom_call" | custom-call | tf_op jit(solution)/shard_map/gather_layer/pallas_call | solution.py:228
  97.3 18.7 all_gather.9
  122.7 29.1 %all-reduce.23.cloned.1.call-done = f32[1,160,1024]{2,1,0:T(8,128)} async-done(((f32[1,160,1024]{2,1,0:T(8,128)}), f32[1,160,1024]{2,1,0:T(8,128)}) %all-reduce.23.cloned.1.call-update) | async-done | bytes 655376 | tf_op jit(solution)/shard_map/psum | solution.py:445
  158.3 3.7 multiply_convert_fusion.5
  168.6 65.7 %gather_layer.4 = bf16[6,1024,1024]{2,1,0:T(8,128)(2,1)} custom-call(bf16[6,64,1024]{2,1,0:T(8,128)(2,1)} %copy-done.81), custom_call_target="tpu_custom_call" | custom-call | tf_op jit(solution)/shard_map/gather_layer/pallas_call | solution.py:228
  244.1 15.2 all_gather.10
  271.0 30.4 %all-reduce.27.cloned.1.call-done = f32[1,160,1024]{2,1,0:T(8,128)} async-done(((f32[1,160,1024]{2,1,0:T(8,128)}), f32[1,160,1024]{2,1,0:T(8,128)}) %all-reduce.27.cloned.1.call-update) | async-done | bytes 655376 | tf_op jit(solution)/shard_map/psum | solution.py:445
  308.4 3.7 multiply_convert_fusion.4
  314.8 3.3 fusion.150
  318.4 66.0 %gather_layer.5 = bf16[6,1024,1024]{2,1,0:T(8,128)(2,1)} custom-call(bf16[6,64,1024]{2,1,0:T(8,128)(2,1)} %copy-done.82), custom_call_target="tpu_custom_call" | custom-call | tf_op jit(solution)/shard_map/gather_layer/pallas_call | solution.py:228
  401.4 14.9 all_gather.11
  430.8 27.0 %all-reduce.31.cloned.1.call-done = f32[1,160,1024]{2,1,0:T(8,128)} async-done(((f32[1,160,1024]{2,1,0:T(8,128)}), f32[1,160,1024]{2,1,0:T(8,128)}) %all-reduce.31.cloned.1.call-update) | async-done | bytes 655376 | tf_op jit(solution)/shard_map/psum | solution.py:445
  464.9 3.8 fusion.325
  479.7 3.3 fusion.174
  483.0 24.7 %all-reduce.33.cloned.1.call-done = f32[1,160,1024]{2,1,0:T(8,128)} async-done(((f32[1,160,1024]{2,1,0:T(8,128)}), f32[1,160,1024]{2,1,0:T(8,128)}) %all-reduce.33.cloned.1.call-update) | async-done | bytes 655376 | tf_op jit(solution)/shard_map/psum | solution.py:445
  528.9 3.5 pad_maximum_fusion.3
  532.3 466.2 %all-reduce.44 = bf16[1,320,1024]{2,0,1:T(2,128)(2,1)} all-reduce(f32[1,320,1024]{2,0,1:T(1,128)} %pad_maximum_fusion.3), channel_id=2, replica_groups=mesh['fsdp'=8,'ctx'=2,'tp'=2] {'ctx'}, use_global_device_ids=true, to_apply=%region_28.29.clone | all-reduce | flops 327680 | bytes 1966080
  1022.7 21.5 all-reduce.35.cloned.1.call-done
  1057.1 3.3 fusion.141
  1066.0 26.7 %all-reduce.37.cloned.1.call-done = f32[1,160,1024]{2,1,0:T(8,128)} async-done(((f32[1,160,1024]{2,1,0:T(8,128)}), f32[1,160,1024]{2,1,0:T(8,128)}) %all-reduce.37.cloned.1.call-update) | async-done | bytes 655376 | tf_op jit(solution)/shard_map/psum | solution.py:445
  1113.2 3.5 pad_maximum_fusion.5
  1116.6 466.4 %all-reduce.45 = bf16[1,320,1024]{2,0,1:T(2,128)(2,1)} all-reduce(f32[1,320,1024]{2,0,1:T(1,128)} %pad_maximum_fusion.5), channel_id=3, replica_groups=mesh['fsdp'=8,'ctx'=2,'tp'=2] {'ctx'}, use_global_device_ids=true, to_apply=%region_36.37.clone | all-reduce | flops 327680 | bytes 1966080
  1593.7 3.3 fusion.192
  1597.1 3.3 maximum_dynamic-update-slice_fusion.1
  1606.7 22.0 all-reduce.39.cloned.1.call-done
  1639.0 3.3 fusion.117
  1646.8 27.7 %all-reduce.41.cloned.1.call-done = f32[1,160,1024]{2,1,0:T(8,128)} async-done(((f32[1,160,1024]{2,1,0:T(8,128)}), f32[1,160,1024]{2,1,0:T(8,128)}) %all-reduce.41.cloned.1.call-update) | async-done | bytes 655376 | tf_op jit(solution)/shard_map/psum | solution.py:445
  1687.8 465.7 %all-reduce.46 = bf16[1,320,1024]{2,0,1:T(2,128)(2,1)} all-reduce(f32[1,320,1024]{2,0,1:T(1,128)S(1)} %pad_maximum_fusion.7), channel_id=4, replica_groups=mesh['fsdp'=8,'ctx'=2,'tp'=2] {'ctx'}, use_global_device_ids=true, to_apply=%region_44.45.clone | all-reduce | flops 327680 | bytes 1966080
  2178.2 32.4 %all-reduce.43.cloned.1.call-done = (f32[1,160,1024]{2,1,0:T(8,128)}, f32[1,160,1024]{2,1,0:T(8,128)}) async-done(((f32[1,160,1024]{2,1,0:T(8,128)}, f32[1,160,1024]{2,1,0:T(8,128)}), (f32[1,160,1024]{2,1,0:T(8,128)}, f32[1,160,1024]{2,1,0:T(8,128)})) %all-reduce.43.cloned.1.call-update) | async-done | bytes 1310736 | tf_op jit(solution)/shard_map/psum | solution.py:445
  2213.6 76.1 %scatter_layer.4 = (f32[6,64,1024]{2,1,0:T(8,128)S(1)}, f32[16,1024]{1,0:T(8,128)S(1)}) custom-call(bf16[6,1024,1024]{2,1,0:T(8,128)(2,1)} %bitcast_dynamic-update-slice_fusion.5.terms_ref, f32[16,1024]{1,0:T(8,128)S(1)} %pad.16.small_ref), custom_call_target="tpu_custom_call" | custom-call | tf_op jit(solution)/shard_map/scatter_layer/pallas_call | solution.py:408
  2289.8 74.8 %scatter_layer.5 = (f32[6,64,1024]{2,1,0:T(8,128)S(1)}, f32[16,1024]{1,0:T(8,128)S(1)}) custom-call(bf16[6,1024,1024]{2,1,0:T(8,128)(2,1)} %bitcast_dynamic-update-slice_fusion.terms_ref, f32[16,1024]{1,0:T(8,128)S(1)} %pad.17.small_ref), custom_call_target="tpu_custom_call" | custom-call | tf_op jit(solution)/shard_map/scatter_layer/pallas_call | solution.py:408
  2364.6 75.8 %scatter_layer.3 = (f32[6,64,1024]{2,1,0:T(8,128)S(1)}, f32[16,1024]{1,0:T(8,128)S(1)}) custom-call(bf16[6,1024,1024]{2,1,0:T(8,128)(2,1)} %bitcast_dynamic-update-slice_fusion.10.terms_ref, f32[16,1024]{1,0:T(8,128)S(1)} %pad.15.small_ref), custom_call_target="tpu_custom_call" | custom-call | tf_op jit(solution)/shard_map/scatter_layer/pallas_call | solution.py:408
  (701 shorter events, 288.6 us)
Async XLA Ops:
  7.3 144.6 %all-reduce.23.cloned.1.call-start = ((), (), s32[]{:S(2)}) async-start(), calls=%async_computation | async-start | bytes 1310720 | tf_op jit(solution)/shard_map/psum | solution.py:445
  10.1 106.4 %copy-start.192 = (pred[320]{0:T(512)(128)(4,1)}, pred[320]{0:T(512)(128)(4,1)S(1)}, u32[]{:S(2)}) copy-start(pred[320]{0:T(512)(128)(4,1)S(1)} %iota_compare_fusion) | copy-start | bytes 964
  11.4 84.1 %copy-start.166 = (f32[160]{0:T(256)}, f32[160]{0:T(256)S(1)}, u32[]{:S(2)}) copy-start(f32[160]{0:T(256)S(1)} %broadcast_multiply_fusion.5) | copy-start | bytes 1924
  11.7 83.8 %copy-start.189 = (f32[160]{0:T(256)}, f32[160]{0:T(256)S(1)}, u32[]{:S(2)}) copy-start(f32[160]{0:T(256)S(1)} %fusion.296) | copy-start | bytes 1924
  15.1 78.7 %copy-start.81 = (bf16[6,64,1024]{2,1,0:T(8,128)(2,1)}, bf16[6,64,1024]{2,1,0:T(8,128)(2,1)S(1)}, u32[]{:S(2)}) copy-start(bf16[6,64,1024]{2,1,0:T(8,128)(2,1)S(1)} %get-tuple-element.158.refs_0_) | copy-start | bytes 2359300
  15.1 78.7 %copy-start.82 = (bf16[6,64,1024]{2,1,0:T(8,128)(2,1)}, bf16[6,64,1024]{2,1,0:T(8,128)(2,1)S(1)}, u32[]{:S(2)}) copy-start(bf16[6,64,1024]{2,1,0:T(8,128)(2,1)S(1)} %get-tuple-element.157.refs_0_) | copy-start | bytes 2359300
  92.2 144.3 %copy-start.123 = (f32[1,1,1024]{2,1,0:T(1,128)}, f32[1,1,1024]{2,1,0:T(1,128)S(1)}, u32[]{:S(2)}) copy-start(f32[1,1,1024]{2,1,0:T(1,128)S(1)} %get-tuple-element.201) | copy-start | bytes 12292
  122.0 112.8 %all-reduce.25.cloned.1.call-start = ((), (), s32[]{:S(2)}) async-start(), calls=%async_computation.1 | async-start | bytes 1310720 | tf_op jit(solution)/shard_map/psum | solution.py:445
  122.7 35.6 %copy-start.118 = (f32[1,2048]{1,0:T(1,128)}, f32[1,2048]{1,0:T(1,128)S(1)}, u32[]{:S(2)}) copy-start(f32[1,2048]{1,0:T(1,128)S(1)} %get-tuple-element.209) | copy-start | bytes 24580
  122.7 185.7 %copy-start.120 = (f32[1,2048]{1,0:T(1,128)}, f32[1,2048]{1,0:T(1,128)S(1)}, u32[]{:S(2)}) copy-start(f32[1,2048]{1,0:T(1,128)S(1)} %get-tuple-element.210) | copy-start | bytes 24580
  168.0 133.4 %all-reduce.27.cloned.1.call-start = ((), (), s32[]{:S(2)}) async-start(), calls=%async_computation.2 | async-start | bytes 1310720 | tf_op jit(solution)/shard_map/psum | solution.py:445
  267.7 33.7 %copy-start.158 = (f32[1,1,1024]{2,1,0:T(1,128)S(1)}, f32[1,1,1024]{2,1,0:T(1,128)}, u32[]{:S(2)}) copy-start(f32[1,1,1024]{2,1,0:T(1,128)} %get-tuple-element.199) | copy-start | bytes 12292
  270.9 32.6 %copy-start.125 = (f32[1,1,1024]{2,1,0:T(1,128)S(1)}, f32[1,1,1024]{2,1,0:T(1,128)}, u32[]{:S(2)}) copy-start(f32[1,1,1024]{2,1,0:T(1,128)} %get-tuple-element.198) | copy-start | bytes 12292
  271.0 32.6 %copy-start.157 = (f32[1,1,1024]{2,1,0:T(1,128)S(1)}, f32[1,1,1024]{2,1,0:T(1,128)}, u32[]{:S(2)}) copy-start(f32[1,1,1024]{2,1,0:T(1,128)} %get-tuple-element.197) | copy-start | bytes 12292
  271.0 120.8 %all-reduce.29.cloned.1.call-start = ((), (), s32[]{:S(2)}) async-start(), calls=%async_computation.3 | async-start | bytes 1310720 | tf_op jit(solution)/shard_map/psum | solution.py:445
  318.1 139.6 %all-reduce.31.cloned.1.call-start = ((), (), s32[]{:S(2)}) async-start(), calls=%async_computation.4 | async-start | bytes 1310720 | tf_op jit(solution)/shard_map/psum | solution.py:445
  318.4 66.0 %copy-start.205 = (u32[32]{0:T(128)S(1)}, u32[32]{0:T(128)}, u32[]{:S(2)}) copy-start(u32[32]{0:T(128)} %constant.137) | copy-start | bytes 388
  427.4 80.4 %all-reduce.33.cloned.1.call-start = ((), (), s32[]{:S(2)}) async-start(), calls=%async_computation.5 | async-start | bytes 1310720 | tf_op jit(solution)/shard_map/psum | solution.py:445
  475.6 568.7 %all-reduce.35.cloned.1.call-start = ((), (), s32[]{:S(2)}) async-start(), calls=%async_computation.6 | async-start | bytes 1310720 | tf_op jit(solution)/shard_map/psum | solution.py:445
  1012.6 80.0 %all-reduce.37.cloned.1.call-start = ((), (), s32[]{:S(2)}) async-start(), calls=%async_computation.7 | async-start | bytes 1310720 | tf_op jit(solution)/shard_map/psum | solution.py:445
  1060.5 568.2 %all-reduce.39.cloned.1.call-start = ((), (), s32[]{:S(2)}) async-start(), calls=%async_computation.8 | async-start | bytes 1310720 | tf_op jit(solution)/shard_map/psum | solution.py:445
  1062.2 32.8 %copy-start.185 = (f32[160]{0:T(256)S(1)}, f32[160]{0:T(256)}, u32[]{:S(2)}) copy-start(f32[160]{0:T(256)} %copy-done.184) | copy-start | bytes 1924
  1597.1 77.5 %all-reduce.41.cloned.1.call-start = ((), (), s32[]{:S(2)}) async-start(), calls=%async_computation.9 | async-start | bytes 1310720 | tf_op jit(solution)/shard_map/psum | solution.py:445
  1630.8 45.6 %copy-start.21 = (f32[1,160,1024]{2,1,0:T(8,128)}, f32[1,160,1024]{2,1,0:T(8,128)S(1)}, u32[]{:S(2)}) copy-start(f32[1,160,1024]{2,1,0:T(8,128)S(1)} %get-tuple-element.126) | copy-start | bytes 1966084
  1642.3 568.2 %all-reduce.43.cloned.1.call-start = ((), (), s32[]{:S(2)}) async-start(), calls=%async_computation.10 | async-start | bytes 2621440 | tf_op jit(solution)/shard_map/psum | solution.py:445
  1643.7 30.9 %copy-start.169 = (f32[160]{0:T(256)S(1)}, f32[160]{0:T(256)}, u32[]{:S(2)}) copy-start(f32[160]{0:T(256)} %copy-done.168) | copy-start | bytes 1924
  1643.7 32.4 %copy-start.181 = (f32[160]{0:T(256)S(1)}, f32[160]{0:T(256)}, u32[]{:S(2)}) copy-start(f32[160]{0:T(256)} %copy-done.180) | copy-start | bytes 1924
  2176.0 34.5 %copy-start.13 = (f32[1,160,1024]{2,1,0:T(8,128)S(1)}, f32[1,160,1024]{2,1,0:T(8,128)}, u32[]{:S(2)}) copy-start(f32[1,160,1024]{2,1,0:T(8,128)} %copy-done.11) | copy-start | bytes 1966084
  2176.0 34.5 %copy-start.16 = (f32[1,160,1024]{2,1,0:T(8,128)S(1)}, f32[1,160,1024]{2,1,0:T(8,128)}, u32[]{:S(2)}) copy-start(f32[1,160,1024]{2,1,0:T(8,128)} %copy-done.14) | copy-start | bytes 1966084
  2176.0 34.5 %copy-start.20 = (f32[1,160,1024]{2,1,0:T(8,128)S(1)}, f32[1,160,1024]{2,1,0:T(8,128)}, u32[]{:S(2)}) copy-start(f32[1,160,1024]{2,1,0:T(8,128)} %get-tuple-element.132) | copy-start | bytes 1966084
  2176.0 34.5 %copy-start.39 = (bf16[1,160,1024]{2,1,0:T(8,128)(2,1)S(1)}, bf16[1,160,1024]{2,1,0:T(8,128)(2,1)}, u32[]{:S(2)}) copy-start(bf16[1,160,1024]{2,1,0:T(8,128)(2,1)} %param.17) | copy-start | bytes 983044
  2176.0 34.5 %copy-start.147 = (f32[160]{0:T(256)S(1)}, f32[160]{0:T(256)}, u32[]{:S(2)}) copy-start(f32[160]{0:T(256)} %copy-done.145) | copy-start | bytes 1924
  (185 other events, 834.9 us)
Sparse Core Ops, SparseCore 0:
  122.2 29.6 all-reduce.22
  168.1 45.9 all-reduce.24
  271.1 30.2 all-reduce.26
  318.3 45.5 all-reduce.28
  427.5 30.2 all-reduce.30
  475.7 32.0 all-reduce.32
  1012.8 31.4 all-reduce.34
  1060.6 32.0 all-reduce.36
  1597.2 31.4 all-reduce.38
  1642.5 32.0 all-reduce.40
  2164.6 45.9 all-reduce.42

commit v2 on v1

--- a/solution.py
+++ b/solution.py
@@ -177,16 +177,11 @@
     return [functools.partial(run, one, two) for one, two in zip(first, second)]
 
 
-def gather_kernel(ctx_size, fsdp_size, with_small, *refs):
-    if with_small:
-        own_ref, small_ref, whole_ref, small_whole, send_sem, recv_sem, local_sem = refs
-    else:
-        own_ref, whole_ref, send_sem, recv_sem, local_sem = refs
-    greet(fsdp_size, ctx_size, False)
-    link = Link(send_sem, recv_sem)
+def gather_events(link, ctx_size, fsdp_size, own_ref, whole_ref, local_sem, small=None):
     both = orders(fsdp_size)
     groups = []
-    if with_small:
+    if small is not None:
+        small_ref, small_whole = small
         groups.append(
             Gather(
                 link, ctx_size, small_ref, small_whole, small_ref.shape[0], both[0], local_sem.at[PARTS]
@@ -209,37 +204,40 @@
                 ]
             )
         )
-    for event in skewed(groups, 1):
+    return skewed(groups, 1)
+
+
+def gather_kernel(ctx_size, fsdp_size, own_ref, small_ref, whole_ref, small_whole, send_sem, recv_sem, local_sem):
+    greet(fsdp_size, ctx_size, False)
+    link = Link(send_sem, recv_sem)
+    small = (small_ref, small_whole)
+    for event in gather_events(link, ctx_size, fsdp_size, own_ref, whole_ref, local_sem, small):
         event()
     link.drain()
 
 
-def gather_layer(mesh, own, small=None):
+def gather_layer(mesh, own, small):
     fsdp_size, ctx_size = mesh.shape["fsdp"], mesh.shape["ctx"]
     parts, block, columns = own.shape
     everyone = fsdp_size * ctx_size
-    out_shape = [jax.ShapeDtypeStruct((parts, everyone * block, columns), own.dtype)]
-    operands = [own]
-    if small is not None:
-        operands.append(small)
-        out_shape.append(jax.ShapeDtypeStruct((everyone * small.shape[0], small.shape[1]), small.dtype))
-    pushes = gather_pushes(fsdp_size, ctx_size) * (parts + len(operands) - 1)
+    pushes = gather_pushes(fsdp_size, ctx_size) * (parts + 1)
     any_space = pl.BlockSpec(memory_space=pl.ANY)
     return pl.pallas_call(
-        functools.partial(gather_kernel, ctx_size, fsdp_size, small is not None),
-        out_shape=out_shape,
-        in_specs=[any_space] * len(operands),
-        out_specs=[any_space] * len(out_shape),
+        functools.partial(gather_kernel, ctx_size, fsdp_size),
+        out_shape=[
+            jax.ShapeDtypeStruct((parts, everyone * block, columns), own.dtype),
+            jax.ShapeDtypeStruct((everyone * small.shape[0], small.shape[1]), small.dtype),
+        ],
+        in_specs=[any_space] * 2,
+        out_specs=[any_space] * 2,
         scratch_shapes=[
             pltpu.SemaphoreType.DMA((pushes,)),
             pltpu.SemaphoreType.DMA((pushes,)),
             pltpu.SemaphoreType.DMA((parts + 1,)),
         ],
-        compiler_params=pltpu.CompilerParams(
-            collective_id=0 if small is None else 1, has_side_effects=True
-        ),
+        compiler_params=pltpu.CompilerParams(collective_id=1, has_side_effects=True),
         name="gather_layer",
-    )(*operands)
+    )(own, small)
 
 
 class Scatter:
@@ -337,16 +335,40 @@
         return [functools.partial(self.step, at) for at in range(len(self.partners) + 1)]
 
 
-def scatter_pushes(fsdp_size):
-    steps = fsdp_size.bit_length() - 2
-    return 2**steps + steps + 1
-
-
-def scatter_kernel(
+def scatter_count(mesh):
+    steps = mesh.shape["fsdp"].bit_length() - 2
+    return (2**steps + steps + 1) * PARTS + steps + 1 + (mesh.shape["ctx"] > 1)
+
+
+def scatter_scratch(mesh, terms, small):
+    parts, depth, columns = terms.shape
+    both = depth // mesh.shape["fsdp"]
+    slots = mesh.shape["fsdp"] // 2
+    steps = mesh.shape["fsdp"].bit_length() - 1 + (mesh.shape["ctx"] > 1)
+    return [
+        pltpu.VMEM((parts, slots, both, columns), BF16),
+        pltpu.VMEM((parts, 2 * slots - 1, both, columns), BF16),
+        pltpu.VMEM((parts, both // mesh.shape["ctx"], columns), BF16),
+        pltpu.VMEM((steps + 1,) + small.shape, F32),
+        pltpu.VMEM((steps,) + small.shape, F32),
+        pltpu.SemaphoreType.DMA((parts, slots)),
+    ]
+
+
+def scatter_shapes(mesh, terms, small):
+    parts, depth, columns = terms.shape
+    block = depth // (mesh.shape["fsdp"] * mesh.shape["ctx"])
+    return [
+        jax.ShapeDtypeStruct((parts, block, columns), F32),
+        jax.ShapeDtypeStruct(small.shape, F32),
+    ]
+
+
+def scatter_events(
+    link,
     ctx_size,
     fsdp_size,
     terms_ref,
-    small_ref,
     out_ref,
     small_out,
     held,
@@ -354,13 +376,8 @@
     last,
     small_held,
     small_arrived,
-    send_sem,
-    recv_sem,
     load_sem,
 ):
-    small_held[0] = small_ref[...]
-    greet(fsdp_size, ctx_size, False)
-    link = Link(send_sem, recv_sem)
     both = [order[::-1] for order in orders(fsdp_size)]
     total = Total(link, fsdp_size, ctx_size, small_held, small_arrived)
     groups = [total.events()]
@@ -390,39 +407,37 @@
                 ]
             )
         )
-    for event in skewed(groups, 1):
+
+    def finish():
+        small_out[...] = small_held[len(total.partners)]
+
+    return skewed(groups, 1), finish
+
+
+def scatter_kernel(ctx_size, fsdp_size, terms_ref, small_ref, out_ref, small_out, *scratch):
+    *buffers, send_sem, recv_sem = scratch
+    buffers[3][0] = small_ref[...]
+    greet(fsdp_size, ctx_size, False)
+    link = Link(send_sem, recv_sem)
+    events, finish = scatter_events(
+        link, ctx_size, fsdp_size, terms_ref, out_ref, small_out, *buffers
+    )
+    for event in events:
         event()
-    small_out[...] = small_held[len(total.partners)]
+    finish()
     link.drain()
 
 
 def scatter_layer(mesh, terms, small):
-    fsdp_size, ctx_size = mesh.shape["fsdp"], mesh.shape["ctx"]
-    parts, depth, columns = terms.shape
-    both = depth // fsdp_size
-    block = both // ctx_size
-    slots = fsdp_size // 2
-    steps = fsdp_size.bit_length() - 1 + (ctx_size > 1)
-    pushes = scatter_pushes(fsdp_size) * parts + steps
+    pushes = scatter_count(mesh)
     vmem = pl.BlockSpec(memory_space=pltpu.VMEM)
     return pl.pallas_call(
-        functools.partial(scatter_kernel, ctx_size, fsdp_size),
-        out_shape=[
-            jax.ShapeDtypeStruct((parts, block, columns), F32),
-            jax.ShapeDtypeStruct(small.shape, F32),
-        ],
+        functools.partial(scatter_kernel, mesh.shape["ctx"], mesh.shape["fsdp"]),
+        out_shape=scatter_shapes(mesh, terms, small),
         in_specs=[pl.BlockSpec(memory_space=pl.ANY), vmem],
         out_specs=[vmem, vmem],
-        scratch_shapes=[
-            pltpu.VMEM((parts, slots, both, columns), BF16),
-            pltpu.VMEM((parts, 2 * slots - 1, both, columns), BF16),
-            pltpu.VMEM((parts, block, columns), BF16),
-            pltpu.VMEM((steps + 1,) + small.shape, F32),
-            pltpu.VMEM((steps,) + small.shape, F32),
-            pltpu.SemaphoreType.DMA((pushes,)),
-            pltpu.SemaphoreType.DMA((pushes,)),
-            pltpu.SemaphoreType.DMA((parts, slots)),
-        ],
+        scratch_shapes=scatter_scratch(mesh, terms, small)
+        + [pltpu.SemaphoreType.DMA((pushes,)), pltpu.SemaphoreType.DMA((pushes,))],
         compiler_params=pltpu.CompilerParams(
             collective_id=2, has_side_effects=True, vmem_limit_bytes=48 * 2**20
         ),
@@ -430,30 +445,543 @@
     )(terms, small)
 
 
-def layer_norm(values, norm_gain, norm_shift):
-    row_mean = jnp.mean(values, axis=-1, keepdims=True)
-    centered = values - row_mean
-    row_var = jnp.mean(centered * centered, axis=-1, keepdims=True)
-    return centered * lax.rsqrt(row_var + EPS) * norm_gain + norm_shift
-
-
-def gelu_exact(values):
-    return jax.nn.gelu(values, approximate=False)
-
-
-def head_sum(partial_rows):
-    return lax.psum(partial_rows, "tp")
-
-
-def dot(spec, left, right):
-    return jnp.einsum(spec, left, right, preferred_element_type=F32)
-
-
-def masked_scores(query_heads, key_heads, key_live, score_scale):
-    raw_scores = dot("nqhd,nkhd->nhqk", query_heads, key_heads) * score_scale
-    return jnp.where(key_live, raw_scores, NEG)
-
-
+def dot_nn(left, right):
+    return lax.dot_general(left, right, (((1,), (0,)), ((), ())), preferred_element_type=F32)
+
+
+def dot_nt(left, right):
+    return lax.dot_general(left, right, (((1,), (1,)), ((), ())), preferred_element_type=F32)
+
+
+def dot_tn(left, right):
+    return lax.dot_general(left, right, (((0,), (0,)), ((), ())), preferred_element_type=F32)
+
+
+TILE = 256
+ROOT_HALF = 0.7071067811865476
+ROOT_TWO_PI = 2.5066282746310002
+GAIN_A, SHIFT_A, OUT_B, GAIN_B, SHIFT_B, DOWN_B, QV_B, UP_B = range(8)
+
+
+def lanes(at, count):
+    return pl.ds(pl.multiple_of(at * count, count), count)
+
+
+def standardized(values):
+    centered = values - jnp.mean(values, axis=-1, keepdims=True)
+    scale = lax.rsqrt(jnp.mean(centered * centered, axis=-1, keepdims=True) + EPS)
+    return centered * scale, scale
+
+
+class Pump:
+    def __init__(self, events):
+        self.events = list(events)
+
+    def __call__(self, count):
+        for event in self.events[:count]:
+            event()
+        self.events = self.events[count:]
+
+    def rest(self):
+        self(len(self.events))
+
+
+def send_pieces(link, partial, sent, got, pieces, partner):
+    copies = []
+    for at in range(pieces):
+        sent[at] = partial(at).astype(BF16)
+        copies.append(link.push(sent.at[at], got.at[at], partner))
+    return copies
+
+
+def both_halves(copies, sent, got):
+    found = []
+    for at, copy in enumerate(copies):
+        copy.wait_recv()
+        found.append(sent[at].astype(F32) + got[at].astype(F32))
+    return jnp.concatenate(found, axis=1)
+
+
+def load_parts(whole_ref, held, load_sem):
+    copies = [
+        pltpu.make_async_copy(whole_ref.at[part], held.at[part], load_sem.at[part])
+        for part in range(PARTS)
+    ]
+    for copy in copies:
+        copy.start()
+    return copies
+
+
+def forward_kernel(ctx_size, fsdp_size, with_next, *refs):
+    refs = list(refs)
+    stream_ref, mask_ref, live_ref, vector_ref, whole_ref = refs[:5]
+    del refs[:5]
+    next_own = refs.pop(0) if with_next else None
+    (
+        out_ref,
+        normed_a_ref,
+        query_ref,
+        kv_ref,
+        log_total_ref,
+        attended_ref,
+        mid_ref,
+        normed_b_ref,
+        pre_ref,
+        hidden_ref,
+    ) = refs[:10]
+    del refs[:10]
+    next_whole = refs.pop(0) if with_next else None
+    held, kv, sent, got, send_sem, recv_sem, load_sem, local_sem = refs
+    rows, width = stream_ref.shape
+    cols = query_ref.shape[1]
+    slots_all = kv.shape[0]
+    pieces = width // TILE
+    ctx = lax.axis_index("ctx")
+    across = {"tp": 1 - lax.axis_index("tp")}
+    loads = load_parts(whole_ref, held, load_sem)
+    greet(fsdp_size, ctx_size, True)
+    link = Link(send_sem, recv_sem)
+    pump = Pump(gather_events(link, ctx_size, fsdp_size, next_own, next_whole, local_sem) if with_next else [])
+    mask = mask_ref[...]
+
+    normal, _ = standardized(stream_ref[...])
+    normed_a_ref[...] = (
+        normal * vector_ref[GAIN_A : GAIN_A + 1, :] + vector_ref[SHIFT_A : SHIFT_A + 1, :]
+    ).astype(BF16)
+    loads[0].wait()
+    loads[1].wait()
+    mine = rows_of(ctx, rows)
+
+    @pl.loop(0, cols // TILE)
+    def _(at):
+        normed = normed_a_ref[...]
+        kv[mine, lanes(at, TILE)] = dot_nn(
+            normed, held[0, :, lanes(at + cols // TILE, TILE)]
+        ).astype(BF16)
+        kv[mine, lanes(at + cols // TILE, TILE)] = (
+            dot_nn(normed, held[1, :, lanes(at, TILE)])
+            + vector_ref[QV_B : QV_B + 1, lanes(at + cols // TILE, TILE)]
+        ).astype(BF16)
+
+    kv_copy = None
+    if ctx_size > 1:
+        kv_copy = link.push(kv.at[mine], kv.at[mine], {"ctx": 1 - ctx})
+    pump(PARTS // 2)
+
+    @pl.loop(0, cols // TILE)
+    def _(at):
+        query_ref[:, lanes(at, TILE)] = (
+            dot_nn(normed_a_ref[...], held[0, :, lanes(at, TILE)])
+            + vector_ref[QV_B : QV_B + 1, lanes(at, TILE)]
+        ).astype(BF16)
+
+    pump(1)
+    if kv_copy is not None:
+        kv_copy.wait_recv()
+    pair = 2 * HEAD_DIM
+    first = lax.broadcasted_iota(jnp.int32, (rows, pair), 1) < HEAD_DIM
+    live = live_ref[...] > 0
+
+    @pl.loop(0, cols // pair)
+    def _(at):
+        queries = query_ref[:, lanes(at, pair)]
+        keys = kv[:, lanes(at, pair)]
+        values = kv[:, lanes(at + cols // pair, pair)]
+        found = []
+        for head in range(2):
+            chosen = jnp.where(first if head == 0 else ~first, queries, jnp.zeros_like(queries))
+            scores = jnp.where(live, dot_nt(chosen, keys) * HEAD_DIM**-0.5, NEG)
+            top = jnp.max(scores, axis=-1, keepdims=True)
+            weights = jnp.exp(scores - top)
+            total = jnp.sum(weights, axis=-1, keepdims=True)
+            log_total_ref[2 * at + head] = top + jnp.log(total)
+            found.append(dot_nn((weights * (1.0 / total)).astype(BF16), values))
+        attended_ref[:, lanes(at, pair)] = jnp.where(first, found[0], found[1]).astype(BF16)
+
+    def out_partial(at):
+        return dot_nt(attended_ref[...], held[1, at * TILE : (at + 1) * TILE, cols:])
+
+    copies = send_pieces(link, out_partial, sent.at[0], got.at[0], pieces, across)
+    kv_ref[...] = kv[...]
+    pump(2)
+    for load in loads[2:]:
+        load.wait()
+    branch = both_halves(copies, sent.at[0], got.at[0])
+    mid = stream_ref[...] + mask * (branch + vector_ref[OUT_B : OUT_B + 1, :])
+    mid_ref[...] = mid
+    normal, _ = standardized(mid)
+    normed_b_ref[...] = (
+        normal * vector_ref[GAIN_B : GAIN_B + 1, :] + vector_ref[SHIFT_B : SHIFT_B + 1, :]
+    ).astype(BF16)
+    pump(2)
+    for part in range(2):
+
+        @pl.loop(0, pieces)
+        def _(at):
+            pre = (
+                dot_nn(normed_b_ref[...], held[2 + part, :, lanes(at, TILE)])
+                + vector_ref[UP_B + part : UP_B + part + 1, lanes(at, TILE)]
+            )
+            pre_ref[part, :, lanes(at, TILE)] = pre
+            hidden_ref[part, :, lanes(at, TILE)] = (
+                0.5 * pre * (1.0 + lax.erf(pre * ROOT_HALF))
+            ).astype(BF16)
+
+    pump(2)
+
+    def down_partial(at):
+        here = slice(at * TILE, (at + 1) * TILE)
+        return dot_nt(hidden_ref[0], held[4, here, :]) + dot_nt(hidden_ref[1], held[5, here, :])
+
+    copies = send_pieces(link, down_partial, sent.at[1], got.at[1], pieces, across)
+    pump(2)
+    branch = both_halves(copies, sent.at[1], got.at[1])
+    out_ref[...] = mid_ref[...] + mask * (branch + vector_ref[DOWN_B : DOWN_B + 1, :])
+    pump.rest()
+    link.drain()
+
+
+def forward_layer(mesh, stream, mask, live, vectors, whole, next_own):
+    fsdp_size, ctx_size = mesh.shape["fsdp"], mesh.shape["ctx"]
+    rows, width = stream.shape
+    cols = width // mesh.shape["tp"]
+    slots_all = rows * ctx_size
+    pieces = width // TILE
+    shape = jax.ShapeDtypeStruct
+    out_shape = [
+        shape((rows, width), F32),
+        shape((rows, width), BF16),
+        shape((rows, cols), BF16),
+        shape((slots_all, 2 * cols), BF16),
+        shape((cols // HEAD_DIM, rows, 1), F32),
+        shape((rows, cols), BF16),
+        shape((rows, width), F32),
+        shape((rows, width), BF16),
+        shape((2, rows, width), F32),
+        shape((2, rows, width), BF16),
+    ]
+    vmem = pl.BlockSpec(memory_space=pltpu.VMEM)
+    any_space = pl.BlockSpec(memory_space=pl.ANY)
+    operands = [stream, mask, live, vectors, whole]
+    in_specs = [vmem] * 4 + [any_space]
+    out_specs = [vmem] * len(out_shape)
+    pushes = (ctx_size > 1) + 2 * pieces
+    with_next = next_own is not None
+    if with_next:
+        operands.append(next_own)
+        in_specs.append(any_space)
+        out_shape.append(shape(whole.shape, BF16))
+        out_specs.append(any_space)
+        pushes += gather_pushes(fsdp_size, ctx_size) * PARTS
+    return pl.pallas_call(
+        functools.partial(forward_kernel, ctx_size, fsdp_size, with_next),
+        out_shape=out_shape,
+        in_specs=in_specs,
+        out_specs=out_specs,
+        scratch_shapes=[
+            pltpu.VMEM(whole.shape, BF16),
+            pltpu.VMEM((slots_all, 2 * cols), BF16),
+            pltpu.VMEM((2, pieces, rows, TILE), BF16),
+            pltpu.VMEM((2, pieces, rows, TILE), BF16),
+            pltpu.SemaphoreType.DMA((pushes,)),
+            pltpu.SemaphoreType.DMA((pushes,)),
+            pltpu.SemaphoreType.DMA((PARTS,)),
+            pltpu.SemaphoreType.DMA((PARTS,)),
+        ],
+        compiler_params=pltpu.CompilerParams(
+            collective_id=3 if with_next else 4,
+            has_side_effects=True,
+            vmem_limit_bytes=56 * 2**20,
+        ),
+        name="forward_layer",
+    )(*operands)
+
+
+def norm_pull(values, gain, grad):
+    normal, scale = standardized(values)
+    grad_gain = jnp.sum(grad * normal, axis=0, keepdims=True)
+    grad_shift = jnp.sum(grad, axis=0, keepdims=True)
+    inner = grad * gain
+    along = jnp.mean(inner * normal, axis=-1, keepdims=True)
+    grad_in = scale * (inner - jnp.mean(inner, axis=-1, keepdims=True) - normal * along)
+    return grad_in, grad_gain, grad_shift
+
+
+def backward_kernel(ctx_size, fsdp_size, with_last, *refs):
+    refs = list(refs)
+    (
+        grad_ref,
+        mask_ref,
+        live_ref,
+        vector_ref,
+        stream_ref,
+        normed_a_ref,
+        query_ref,
+        kv_ref,
+        log_total_ref,
+        attended_ref,
+        mid_ref,
+        normed_b_ref,
+        pre_ref,
+        hidden_ref,
+        whole_ref,
+    ) = refs[:15]
+    del refs[:15]
+    if with_last:
+        last_terms, last_small = refs[:2]
+        del refs[:2]
+    out_ref, small_ref, terms_ref = refs[:3]
+    del refs[:3]
+    if with_last:
+        summed_ref, small_summed = refs[:2]
+        del refs[:2]
+    (
+        held,
+        terms,
+        turned,
+        low,
+        low_pre,
+        grad_att,
+        grad_qk,
+        grad_kv,
+        kv_sent,
+        kv_got,
+        sent,
+        got,
+        send_sem,
+        recv_sem,
+        load_sem,
+        term_sem,
+    ) = refs[:16]
+    del refs[:16]
+    rows, width = grad_ref.shape
+    cols = query_ref.shape[1]
+    pieces = width // TILE
+    ctx = lax.axis_index("ctx")
+    across = {"tp": 1 - lax.axis_index("tp")}
+    loads = load_parts(whole_ref, held, load_sem)
+    small_ref[...] = jnp.zeros_like(small_ref)
+    if with_last:
+        small_held = refs[3]
+        small_held[0] = last_small[...]
+    greet(fsdp_size, ctx_size, True)
+    link = Link(send_sem, recv_sem)
+    pump = Pump([])
+    if with_last:
+        events, finish = scatter_events(
+            link, ctx_size, fsdp_size, last_terms, summed_ref, small_summed, *refs
+        )
+        pump = Pump(events)
+    mask = mask_ref[...]
+    stores = []
+
+    def keep(part):
+        copy = pltpu.make_async_copy(terms.at[part], terms_ref.at[part], term_sem.at[part])
+        copy.start()
+        stores.append(copy)
+
+    def product(part, start, count, right):
+        @pl.loop(0, count)
+        def _(at):
+            terms[part, :, lanes(at + start, TILE)] = dot_nn(turned[...], right(at)).astype(BF16)
+
+    masked = mask * grad_ref[...]
+    small_ref[DOWN_B : DOWN_B + 1, :] = jnp.sum(masked, axis=0, keepdims=True)
+    low[...] = masked.astype(BF16)
+    pump(PARTS // 2 + 1)
+    for load in loads:
+        load.wait()
+    for part in range(2):
+
+        @pl.loop(0, pieces)
+        def _(at):
+            pre = pre_ref[part, :, lanes(at, TILE)]
+            slope = 0.5 * (1.0 + lax.erf(pre * ROOT_HALF)) + pre * (
+                jnp.exp(-0.5 * pre * pre) * (1.0 / ROOT_TWO_PI)
+            )
+            grad_pre = dot_nn(low[...], held[4 + part, :, lanes(at, TILE)]) * slope
+            small_ref[UP_B + part : UP_B + part + 1, lanes(at, TILE)] = jnp.sum(
+                grad_pre, axis=0, keepdims=True
+            )
+            low_pre[part, :, lanes(at, TILE)] = grad_pre.astype(BF16)
+
+    def up_partial(at):
+        here = slice(at * TILE, (at + 1) * TILE)
+        return dot_nt(low_pre[0], held[2, here, :]) + dot_nt(low_pre[1], held[3, here, :])
+
+    copies = send_pieces(link, up_partial, sent.at[0], got.at[0], pieces, across)
+    pump(2)
+    turned[...] = jnp.transpose(low[...])
+    for part in range(2):
+        product(4 + part, 0, pieces, lambda at, part=part: hidden_ref[part, :, lanes(at, TILE)])
+        keep(4 + part)
+    turned[...] = jnp.transpose(normed_b_ref[...])
+    for part in range(2):
+        product(2 + part, 0, pieces, lambda at, part=part: low_pre[part, :, lanes(at, TILE)])
+        keep(2 + part)
+    pump(2)
+    grad_normed = both_halves(copies, sent.at[0], got.at[0])
+    grad_in, grad_gain, grad_shift = norm_pull(
+        mid_ref[...], vector_ref[GAIN_B : GAIN_B + 1, :], grad_normed
+    )
+    small_ref[GAIN_B : GAIN_B + 1, :] = grad_gain
+    small_ref[SHIFT_B : SHIFT_B + 1, :] = grad_shift
+    grad_mid = grad_ref[...] + grad_in
+    out_ref[...] = grad_mid
+    masked = mask * grad_mid
+    small_ref[OUT_B : OUT_B + 1, :] = jnp.sum(masked, axis=0, keepdims=True)
+    low[...] = masked.astype(BF16)
+
+    @pl.loop(0, cols // TILE)
+    def _(at):
+        grad_att[:, lanes(at, TILE)] = dot_nn(
+            low[...], held[1, :, lanes(at + cols // TILE, TILE)]
+        ).astype(BF16)
+
+    pump(2)
+    pair = 2 * HEAD_DIM
+    first = lax.broadcasted_iota(jnp.int32, (rows, pair), 1) < HEAD_DIM
+    live = live_ref[...] > 0
+
+    @pl.loop(0, cols // pair)
+    def _(at):
+        queries = query_ref[:, lanes(at, pair)]
+        grads = grad_att[:, lanes(at, pair)]
+        keys = kv_ref[:, lanes(at, pair)]
+        values = kv_ref[:, lanes(at + cols // pair, pair)]
+        found, key_grad, value_grad = [], None, None
+        for head in range(2):
+            here = first if head == 0 else ~first
+            query = jnp.where(here, queries, jnp.zeros_like(queries))
+            grad = jnp.where(here, grads, jnp.zeros_like(grads))
+            scores = jnp.where(live, dot_nt(query, keys) * HEAD_DIM**-0.5, NEG)
+            weights = jnp.exp(scores - log_total_ref[2 * at + head])
+            grad_weights = dot_nt(grad, values)
+            along = jnp.sum(weights * grad_weights, axis=-1, keepdims=True)
+            grad_scores = (weights * (grad_weights - along)).astype(BF16)
+            found.append(dot_nn(grad_scores, keys))
+            one = dot_tn(grad_scores, query)
+            two = dot_tn(weights.astype(BF16), grad)
+            key_grad = one if head == 0 else key_grad + one
+            value_grad = two if head == 0 else value_grad + two
+        grad_qk[:, lanes(at, pair)] = (
+            jnp.where(first, found[0], found[1]) * HEAD_DIM**-0.5
+        ).astype(BF16)
+        grad_kv[:, lanes(at, pair)] = key_grad * HEAD_DIM**-0.5
+        grad_kv[:, lanes(at + cols // pair, pair)] = value_grad
+
+    mine, theirs = rows_of(ctx, rows), rows_of(1 - ctx, rows)
+    kv_copy = None
+    if ctx_size > 1:
+        kv_sent[...] = grad_kv[theirs, :].astype(BF16)
+        kv_copy = link.push(kv_sent, kv_got, {"ctx": 1 - ctx})
+    pump(2)
+    small_ref[QV_B : QV_B + 1, :cols] = jnp.sum(
+        grad_qk[:, :cols].astype(F32), axis=0, keepdims=True
+    )
+    turned[...] = jnp.transpose(low[...])
+    product(1, cols // TILE, cols // TILE, lambda at: attended_ref[:, lanes(at, TILE)])
+    turned[...] = jnp.transpose(normed_a_ref[...])
+    product(0, 0, cols // TILE, lambda at: grad_qk[:, lanes(at, TILE)])
+    pump(1)
+    total_kv = grad_kv[mine, :]
+    if kv_copy is not None:
+        kv_copy.wait_recv()
+        total_kv = total_kv + kv_got[...].astype(F32)
+    total_kv = total_kv.astype(BF16)
+    grad_qk[:, cols:] = total_kv
+    small_ref[QV_B : QV_B + 1, cols:] = jnp.sum(
+        grad_qk[:, 2 * cols :].astype(F32), axis=0, keepdims=True
+    )
+
+    def in_partial(at):
+        here = slice(at * TILE, (at + 1) * TILE)
+        return dot_nt(grad_qk[:, : 2 * cols], held[0, here, :]) + dot_nt(
+            grad_qk[:, 2 * cols :], held[1, here, :cols]
+        )
+
+    copies = send_pieces(link, in_partial, sent.at[1], got.at[1], pieces, across)
+    product(0, cols // TILE, cols // TILE, lambda at: grad_qk[:, lanes(at + cols // TILE, TILE)])
+    keep(0)
+    product(1, 0, cols // TILE, lambda at: grad_qk[:, lanes(at + 2 * cols // TILE, TILE)])
+    keep(1)
+    pump(2)
+    grad_normed = both_halves(copies, sent.at[1], got.at[1])
+    grad_in, grad_gain, grad_shift = norm_pull(
+        stream_ref[...], vector_ref[GAIN_A : GAIN_A + 1, :], grad_normed
+    )
+    small_ref[GAIN_A : GAIN_A + 1, :] = grad_gain
+    small_ref[SHIFT_A : SHIFT_A + 1, :] = grad_shift
+    out_ref[...] = out_ref[...] + grad_in
+    pump.rest()
+    if with_last:
+        finish()
+    for copy in stores:
+        copy.wait()
+    link.drain()
+
+
+def backward_layer(mesh, grad, mask, live, vectors, kept, whole, last):
+    fsdp_size, ctx_size = mesh.shape["fsdp"], mesh.shape["ctx"]
+    rows, width = grad.shape
+    cols = width // mesh.shape["tp"]
+    slots_all = rows * ctx_size
+    pieces = width // TILE
+    shape = jax.ShapeDtypeStruct
+    vmem = pl.BlockSpec(memory_space=pltpu.VMEM)
+    any_space = pl.BlockSpec(memory_space=pl.ANY)
+    operands = [grad, mask, live, vectors, *kept, whole]
+    in_specs = [vmem] * (len(operands) - 1) + [any_space]
+    out_shape = [
+        shape((rows, width), F32),
+        shape(vectors.shape, F32),
+        shape(whole.shape, BF16),
+    ]
+    out_specs = [vmem, vmem, any_space]
+    pushes = (ctx_size > 1) + 2 * pieces
+    scratch = [
+        pltpu.VMEM(whole.shape, BF16),
+        pltpu.VMEM(whole.shape, BF16),
+        pltpu.VMEM((width, rows), BF16),
+        pltpu.VMEM((rows, width), BF16),
+        pltpu.VMEM((2, rows, width), BF16),
+        pltpu.VMEM((rows, cols), BF16),
+        pltpu.VMEM((rows, 3 * cols), BF16),
+        pltpu.VMEM((slots_all, 2 * cols), F32),
+        pltpu.VMEM((rows, 2 * cols), BF16),
+        pltpu.VMEM((rows, 2 * cols), BF16),
+        pltpu.VMEM((2, pieces, rows, TILE), BF16),
+        pltpu.VMEM((2, pieces, rows, TILE), BF16),
+    ]
+    with_last = last is not None
+    if with_last:
+        last_terms, last_small = last
+        operands += [last_terms, last_small]
+        in_specs += [any_space, vmem]
+        out_shape += scatter_shapes(mesh, last_terms, last_small)
+        out_specs += [vmem, vmem]
+        pushes += scatter_count(mesh)
+    scratch += [
+        pltpu.SemaphoreType.DMA((pushes,)),
+        pltpu.SemaphoreType.DMA((pushes,)),
+        pltpu.SemaphoreType.DMA((PARTS,)),
+        pltpu.SemaphoreType.DMA((PARTS,)),
+    ]
+    if with_last:
+        scratch += scatter_scratch(mesh, last_terms, last_small)
+    return pl.pallas_call(
+        functools.partial(backward_kernel, ctx_size, fsdp_size, with_last),
+        out_shape=out_shape,
+        in_specs=in_specs,
+        out_specs=out_specs,
+        scratch_shapes=scratch,
+        compiler_params=pltpu.CompilerParams(
+            collective_id=5 if with_last else 6,
+            has_side_effects=True,
+            vmem_limit_bytes=62 * 2**20,
+        ),
+        name="backward_layer",
+    )(*operands)
 def body(
     mesh,
     tokens,
@@ -475,16 +1003,12 @@
     images, local_slots, width = tokens.shape
     fsdp_size, ctx_size = mesh.shape["fsdp"], mesh.shape["ctx"]
     everyone = fsdp_size * ctx_size
-    slots_all = local_slots * ctx_size
+    rows_here, slots_all = images * local_slots, local_slots * ctx_size
     layers, block, _, cols = qkv_weight.shape
-    heads_here = cols // HEAD_DIM
     units = up_weight.shape[2]
-    score_scale = HEAD_DIM ** (-0.5)
     slot_ids = lax.axis_index("ctx") * local_slots + jnp.arange(local_slots, dtype=jnp.int32)
-    row_mask = (slot_ids[None, :] < lengths[:, None]).astype(F32)[:, :, None]
-    key_live = (jnp.arange(slots_all, dtype=jnp.int32)[None, :] < lengths[:, None])[
-        :, None, None, :
-    ]
+    mask = (slot_ids[None, :] < lengths[:, None]).astype(F32).reshape(rows_here, 1)
+    live = (jnp.arange(slots_all, dtype=jnp.int32)[None, :] < lengths[:, None]).astype(F32)
     vectors = jnp.stack((attn_gain, attn_shift, out_bias, mlp_gain, mlp_shift, down_bias), axis=1)
     flat = vectors.reshape(-1)
     small_rows = 16 * -(-flat.size // (16 * 2 * cols))
@@ -504,154 +1028,40 @@
             )
         )
 
-    weights = []
+    whole, small_whole = gather_layer(mesh, own_parts(0), small)
+    gathered = small_whole.reshape(everyone, small_rows * 2 * cols)[:, : flat.size]
+    gathered = jnp.swapaxes(gathered.reshape(everyone, layers * 6, block), 0, 1)
+    vectors = jnp.concatenate(
+        (
+            gathered.reshape(layers, 6, width),
+            qv_bias.reshape(layers, 1, width),
+            up_bias.reshape(layers, units // width, width),
+        ),
+        axis=1,
+    ).astype(F32)
+    vectors = jnp.pad(vectors, ((0, 0), (0, -vectors.shape[1] % 8), (0, 0)))
+
+    stream = tokens.astype(F32).reshape(rows_here, width) * mask
+    kept, weights = [], []
     for at in range(layers):
-        if at == 0:
-            whole, small_whole = gather_layer(mesh, own_parts(at), small)
-        else:
-            (whole,) = gather_layer(mesh, own_parts(at))
         weights.append(whole)
-    gathered = small_whole.reshape(everyone, small_rows * 2 * cols)[:, : flat.size]
-    vectors = jnp.swapaxes(gathered.reshape(everyone, layers * 6, block), 0, 1)
-    vectors = vectors.reshape(layers, 6, width).astype(F32)
-
-    stream = tokens.astype(F32) * row_mask
-    kept = []
-    for at in range(layers):
-        whole = weights[at]
-        gain_a, shift_a, out_b, gain_b, shift_b, down_b = [vectors[at, i] for i in range(6)]
-        bias_qv = qv_bias[at].astype(F32)
-        normed_a = layer_norm(stream, gain_a, shift_a).astype(BF16)
-        queries = (dot("nsd,df->nsf", normed_a, whole[0, :, :cols]) + bias_qv[0]).astype(BF16)
-        keys_own = dot("nsd,df->nsf", normed_a, whole[0, :, cols:]).astype(BF16)
-        values_own = (dot("nsd,df->nsf", normed_a, whole[1, :, :cols]) + bias_qv[1]).astype(BF16)
-        both = lax.all_gather(jnp.concatenate((keys_own, values_own), -1), "ctx", axis=1, tiled=True)
-        query_heads = queries.reshape(images, local_slots, heads_here, HEAD_DIM)
-        key_heads = both[:, :, :cols].reshape(images, slots_all, heads_here, HEAD_DIM)
-        value_heads = both[:, :, cols:].reshape(images, slots_all, heads_here, HEAD_DIM)
-        scores = masked_scores(query_heads, key_heads, key_live, score_scale)
-        row_top = jnp.max(scores, axis=-1, keepdims=True)
-        exp_scores = jnp.exp(scores - row_top)
-        row_total = jnp.sum(exp_scores, axis=-1, keepdims=True)
-        attn_probs = (exp_scores / row_total).astype(BF16)
-        log_total = row_top + jnp.log(row_total)
-        attended = dot("nhqk,nkhd->nqhd", attn_probs, value_heads)
-        attended = attended.reshape(images, local_slots, cols).astype(BF16)
-        branch_a = head_sum(dot("nsf,df->nsd", attended, whole[1, :, cols:]))
-        mid = stream + row_mask * (branch_a + out_b)
-        normed_b = layer_norm(mid, gain_b, shift_b).astype(BF16)
-        hidden_pre = jnp.concatenate(
-            [dot("nsd,df->nsf", normed_b, whole[part]) for part in (2, 3)], axis=-1
-        ) + up_bias[at].astype(F32)
-        hidden = gelu_exact(hidden_pre).astype(BF16)
-        halves = (hidden[:, :, : units // 2], hidden[:, :, units // 2 :])
-        branch_b = head_sum(
-            dot("nsf,df->nsd", halves[0], whole[4]) + dot("nsf,df->nsd", halves[1], whole[5])
-        )
-        kept.append(
-            (
-                stream,
-                normed_a,
-                query_heads,
-                key_heads,
-                value_heads,
-                log_total,
-                attended,
-                mid,
-                normed_b,
-                hidden_pre,
-                halves,
-            )
-        )
-        stream = mid + row_mask * (branch_b + down_b)
-    output = stream.astype(BF16)
-    grad_stream = cotangent.astype(F32)
+        next_own = own_parts(at + 1) if at + 1 < layers else None
+        found = forward_layer(mesh, stream, mask, live, vectors[at], whole, next_own)
+        kept.append((stream, *found[1:10]))
+        stream = found[0]
+        whole = found[-1]
+    output = stream.astype(BF16).reshape(tokens.shape)
+    grad = cotangent.astype(F32).reshape(rows_here, width)
     big, little = [None] * layers, [None] * layers
+    last = None
     for at in reversed(range(layers)):
-        (
-            layer_in,
-            normed_a,
-            query_heads,
-            key_heads,
-            value_heads,
-            log_total,
-            attended,
-            mid,
-            normed_b,
-            hidden_pre,
-            halves,
-        ) = kept[at]
-        whole = weights[at]
-        gain_a, shift_a, out_b, gain_b, shift_b, down_b = [vectors[at, i] for i in range(6)]
-        grad_branch_b = row_mask * grad_stream
-        grad_down_b = jnp.sum(grad_branch_b, axis=(0, 1))
-        low_b = grad_branch_b.astype(BF16)
-        grad_down = [dot("nsd,nsf->df", low_b, half) for half in halves]
-        grad_hidden = jnp.concatenate(
-            [dot("nsd,df->nsf", low_b, whole[part]) for part in (4, 5)], axis=-1
-        )
-        grad_pre = jax.vjp(gelu_exact, hidden_pre)[1](grad_hidden)[0]
-        grad_up_b = jnp.sum(grad_pre, axis=(0, 1))
-        low_pre = grad_pre.astype(BF16)
-        pre_halves = (low_pre[:, :, : units // 2], low_pre[:, :, units // 2 :])
-        grad_up = [dot("nsd,nsf->df", normed_b, half) for half in pre_halves]
-        grad_normed_b = head_sum(
-            dot("nsf,df->nsd", pre_halves[0], whole[2])
-            + dot("nsf,df->nsd", pre_halves[1], whole[3])
-        )
-        grad_mid_norm, grad_gain_b, grad_shift_b = jax.vjp(layer_norm, mid, gain_b, shift_b)[1](
-            grad_normed_b
-        )
-        grad_mid = grad_stream + grad_mid_norm
-        grad_branch_a = row_mask * grad_mid
-        grad_out_b = jnp.sum(grad_branch_a, axis=(0, 1))
-        low_a = grad_branch_a.astype(BF16)
-        grad_out = dot("nsd,nsf->df", low_a, attended)
-        grad_att = dot("nsd,df->nsf", low_a, whole[1, :, cols:]).astype(BF16)
-        grad_att = grad_att.reshape(images, local_slots, heads_here, HEAD_DIM)
-        scores = masked_scores(query_heads, key_heads, key_live, score_scale)
-        attn_p = jnp.exp(scores - log_total)
-        grad_probs = dot("nqhd,nkhd->nhqk", grad_att, value_heads)
-        row_dot = jnp.sum(attn_p * grad_probs, axis=-1, keepdims=True)
-        grad_scores = (attn_p * (grad_probs - row_dot)).astype(BF16)
-        grad_q = (dot("nhqk,nkhd->nqhd", grad_scores, key_heads) * score_scale).astype(BF16)
-        grad_q = grad_q.reshape(images, local_slots, cols)
-        grad_k = dot("nhqk,nqhd->nkhd", grad_scores, query_heads) * score_scale
-        grad_v = dot("nhqk,nqhd->nkhd", attn_p.astype(BF16), grad_att)
-        grad_kv = jnp.concatenate(
-            (
-                grad_k.reshape(images, slots_all, cols),
-                grad_v.reshape(images, slots_all, cols),
-            ),
-            axis=-1,
-        )
-        grad_kv = lax.psum_scatter(grad_kv, "ctx", scatter_dimension=1, tiled=True).astype(BF16)
-        grad_v = grad_kv[:, :, cols:]
-        grad_qv_b = jnp.concatenate(
-            (jnp.sum(grad_q.astype(F32), axis=(0, 1)), jnp.sum(grad_v.astype(F32), axis=(0, 1)))
-        )
-        grad_qk = jnp.concatenate((grad_q, grad_kv[:, :, :cols]), axis=-1)
-        terms = [
-            dot("nsd,nsf->df", normed_a, grad_qk),
-            jnp.concatenate((dot("nsd,nsf->df", normed_a, grad_v), grad_out), axis=1),
-            *grad_up,
-            *grad_down,
-        ]
-        grad_normed_a = head_sum(
-            dot("nsf,df->nsd", grad_qk, whole[0]) + dot("nsf,df->nsd", grad_v, whole[1, :, :cols])
-        )
-        grad_in_norm, grad_gain_a, grad_shift_a = jax.vjp(layer_norm, layer_in, gain_a, shift_a)[1](
-            grad_normed_a
-        )
-        grad_stream = grad_mid + grad_in_norm
-        rows = [grad_gain_a, grad_shift_a, grad_out_b, grad_gain_b, grad_shift_b, grad_down_b]
-        rows.append(grad_qv_b)
-        rows.extend(jnp.split(grad_up_b, units // width))
-        rows = jnp.pad(jnp.stack(rows), ((0, -len(rows) % 8), (0, 0)))
-        big[at], little[at] = scatter_layer(
-            mesh, jnp.stack([term.astype(BF16) for term in terms]), rows
-        )
-    input_grad = grad_stream * row_mask
+        found = backward_layer(mesh, grad, mask, live, vectors[at], kept[at], weights[at], last)
+        grad = found[0]
+        if last is not None:
+            big[at + 1], little[at + 1] = found[3:]
+        last = (found[2], found[1])
+    big[0], little[0] = scatter_layer(mesh, *last)
+    input_grad = (grad * mask).reshape(tokens.shape)
     big, little = jnp.stack(big), jnp.stack(little)
     here = (lax.axis_index("fsdp") * ctx_size + lax.axis_index("ctx")) * block
     own_vectors = lax.dynamic_slice_in_dim(little[:, :6], here, block, axis=2)

time: 2480 us -> 642 us (0.26)
  blocking collectives: 1450 us -> 0 us
  waiting for transfers between devices: 242 us -> 0 us
  matrix products: 182 us -> 0 us
  Pallas kernels: 433 us -> 608 us
  other arithmetic: 82.2 us -> 14.5 us
  local copies, waits for them, and re-layouts: 60.3 us -> 14.8 us
    unnamed x3 -> x0, blocking collectives: 1400 us -> none
    psum x11 -> x0, waiting for transfers between devices: 241 us -> none  [head_sum(): return lax.psum(partial_rows, 'tp')]
    dot_general x84 -> x0, matrix products: 182 us -> none  [dot(): return jnp.einsum(spec, left, right, preferred_element_type=F32)]
    pallas_call x6 -> x8, Pallas kernels: 433 us -> 608 us  [the longest x3 231 us: backward_layer(): pl.pallas_call(functools.partial(backward_kernel, ctx_size, fsdp_size, wi...]
    all_gather x3 -> x0, blocking collectives: 48.8 us -> none  [body(): lax.all_gather(jnp.concatenate((keys_own, values_own), -1), 'ctx', axis=1...]
    reduce_sum x33 -> x0, other arithmetic: 37.5 us -> none  [the longest x6 12.4 us: layer_norm(): return centered * lax.rsqrt(row_var + EPS) * norm_gain + norm_shift]
  transfers between devices with their start and end apart: 11 -> 0, of which waited for: 9 -> 0; matrix products, arithmetic and copies ran while one was open for 2% -> 0% of each run, Pallas kernels for 5% -> 0%
where the time goes in v2:
time: 642 us; the launch traced here: 639 us
  Pallas kernels  608 us (95%)
  local copies, waits for them, and re-layouts  14.8 us (2%)
  other arithmetic  14.5 us (2%)
    pallas_call x3, Pallas kernels, backward_layer(): pl.pallas_call(functools.partial(backward_kernel, ctx_size, fsdp_size, wi...  231 us
    pallas_call x3, Pallas kernels, forward_layer(): pl.pallas_call(functools.partial(forward_kernel, ctx_size, fsdp_size, wit...  228 us
    pallas_call x1, Pallas kernels, gather_layer(): pl.pallas_call(functools.partial(gather_kernel, ctx_size, fsdp_size), out...  74.8 us
    pallas_call x1, Pallas kernels, scatter_layer(): pl.pallas_call(functools.partial(scatter_kernel, mesh.shape['ctx'], mesh....  73.6 us

profile of v2, /device:TPU:0, one launch (start us, length us, event | category | flops | bytes accessed | tf_op | source)
XLA Modules:
  0.0 638.9 jit_solution(5746738076956041529)
XLA Ops:
  1.4 1.9 convert_multiply_fusion.refs_0_.refs_4_
  3.3 0.6 fusion.9.refs_1_
  4.5 0.7 reshape.114
  5.2 0.7 reshape.125
  5.9 1.1 slice_bitcast_fusion.1
  7.1 1.0 slice_bitcast_fusion.10
  8.4 0.9 copy-done.7
  9.6 0.9 reshape.109.small_ref
  10.5 74.8 %gather_layer.1 = (bf16[6,1024,1024]{2,1,0:T(8,128)(2,1)}, bf16[256,1024]{1,0:T(8,128)(2,1)}) custom-call(bf16[6,64,1024]{2,1,0:T(8,128)(2,1)} %copy-done.5, bf16[16,1024]{1,0:T(8,128)(2,1)} %reshape.109.small_ref), custom_call_target="tpu_custom_call" | custom-call | tf_op jit(solution)/shard_map/gather_layer/pallas_call | solution.py:225
  85.4 1.3 reshape.110
  87.0 0.7 slice_bitcast_fusion.4
  87.7 91.7 %forward_layer.3 = (f32[160,1024]{1,0:T(8,128)}, bf16[160,1024]{1,0:T(8,128)(2,1)}, bf16[160,512]{1,0:T(8,128)(2,1)}, bf16[320,1024]{1,0:T(8,128)(2,1)}, f32[8,1...) custom-call(f32[160,1024]{1,0:T(8,128)} %convert_multiply_fusion.ref, ...), custom_call_target="tpu_custom_call" | custom-call | tf_op jit(solution)/shard_map/forward_layer/pallas_call | solution.py:676
  179.3 89.8 %forward_layer.4 = (f32[160,1024]{1,0:T(8,128)}, bf16[160,1024]{1,0:T(8,128)(2,1)}, bf16[160,512]{1,0:T(8,128)(2,1)}, bf16[320,1024]{1,0:T(8,128)(2,1)}, f32[8,1...) custom-call(f32[160,1024]{1,0:T(8,128)} %get-tuple-element.65.refs_0, ...), custom_call_target="tpu_custom_call" | custom-call | tf_op jit(solution)/shard_map/forward_layer/pallas_call | solution.py:676
  269.1 46.8 %forward_layer.5 = (f32[160,1024]{1,0:T(8,128)}, bf16[160,1024]{1,0:T(8,128)(2,1)}, bf16[160,512]{1,0:T(8,128)(2,1)}, bf16[320,1024]{1,0:T(8,128)(2,1)}, f32[8,1...) custom-call(f32[160,1024]{1,0:T(8,128)} %get-tuple-element.67.refs_0, ...), custom_call_target="tpu_custom_call" | custom-call | tf_op jit(solution)/shard_map/forward_layer/pallas_call | solution.py:676
  316.0 1.9 convert_bitcast_fusion
  317.8 0.9 bitcast_convert_fusion.refs_0_
  318.7 44.3 %backward_layer.3 = (f32[160,1024]{1,0:T(8,128)}, f32[16,1024]{1,0:T(8,128)}, bf16[6,1024,1024]{2,1,0:T(8,128)(2,1)}) custom-call(f32[160,1024]{1,0:T(8,128)} %bitcast_convert_fusion.refs_0_, f32[160,1]{1,0:T(8,128)} %fusion.9.refs_1_, f32[1,320]{1,0:T(1,128)} %compare_convert_fusion.refs_2_, f32[16,1024]{1,0:T(8,128)} %get-tuple-element.164.refs_3_, ...), custom_call_target="tpu_custom_call" | custom-call | tf_op jit(solution)/shard_map/backward_layer/pallas_call | solution.py:972
  363.0 93.9 %backward_layer.4 = (f32[160,1024]{1,0:T(8,128)}, f32[16,1024]{1,0:T(8,128)}, bf16[6,1024,1024]{2,1,0:T(8,128)(2,1)}, f32[6,64,1024]{2,1,0:T(8,128)}, f32[16,1024]{1,0:T(8,128)}) custom-call(f32[160,1024]{1,0:T(8,128)} %get-tuple-element.79.refs_0_, f32[160,1]{1,0:T(8,128)} %fusion.9.refs_1_, f32[1,320]{1,0:T(1,128)} %compare_convert_fusion.refs_2_, ...), custom_call_target="tpu_custom_call" | custom-call | tf_op jit(solution)/shard_map/backward_layer/pallas_call | solution.py:972
  456.9 92.8 %backward_layer.5 = (f32[160,1024]{1,0:T(8,128)}, f32[16,1024]{1,0:T(8,128)}, bf16[6,1024,1024]{2,1,0:T(8,128)(2,1)}, f32[6,64,1024]{2,1,0:T(8,128)}, f32[16,1024]{1,0:T(8,128)}) custom-call(f32[160,1024]{1,0:T(8,128)} %get-tuple-element.91.refs_0_, f32[160,1]{1,0:T(8,128)} %fusion.9.refs_1_, f32[1,320]{1,0:T(1,128)} %compare_convert_fusion.refs_2_, ...), custom_call_target="tpu_custom_call" | custom-call | tf_op jit(solution)/shard_map/backward_layer/pallas_call | solution.py:972
  549.7 2.0 multiply_bitcast_fusion
  551.8 0.8 copy-done
  552.6 73.6 %scatter_layer.1 = (f32[6,64,1024]{2,1,0:T(8,128)S(1)}, f32[16,1024]{1,0:T(8,128)S(1)}) custom-call(bf16[6,1024,1024]{2,1,0:T(8,128)(2,1)} %get-tuple-element.104.terms_ref, f32[16,1024]{1,0:T(8,128)S(1)} %copy-done), custom_call_target="tpu_custom_call" | custom-call | tf_op jit(solution)/shard_map/scatter_layer/pallas_call | solution.py:434
  626.4 0.6 copy.70
  627.0 0.6 copy.69
  627.5 1.9 maximum_bitcast_fusion.5
  630.1 1.1 copy.64
  631.2 0.6 reshape_squeeze.3
  632.5 0.6 copy.67
  633.6 1.4 maximum_bitcast_fusion.2
  635.0 1.2 pad_maximum_fusion.1
  636.3 0.6 copy.56
  636.9 1.2 maximum_bitcast_fusion
  (74 shorter events, 3.9 us)
Async XLA Ops:
  0.6 6.4 %copy-start.11 = (bf16[3,512,64]{1,2,0:T(8,128)(2,1)S(1)}, bf16[3,512,64]{1,2,0:T(8,128)(2,1)}, u32[]{:S(2)}) copy-start(bf16[3,512,64]{1,2,0:T(8,128)(2,1)} %param.22) | copy-start | bytes 589828
  7.0 1.2 copy-start.6
  8.1 1.2 copy-start.7
  8.2 1.1 copy-start.12
  8.2 1.2 copy-start.13
  8.2 1.2 copy-start.14
  8.2 1.2 copy-start.15
  8.3 1.2 copy-start.16
  8.3 1.2 copy-start.17
  9.3 1.2 copy-start.5
  9.3 78.3 %copy-start.3 = (bf16[6,64,1024]{2,1,0:T(8,128)(2,1)}, bf16[6,64,1024]{2,1,0:T(8,128)(2,1)S(1)}, u32[]{:S(2)}) copy-start(bf16[6,64,1024]{2,1,0:T(8,128)(2,1)S(1)} %get-tuple-element.147.refs_5_) | copy-start | bytes 2359300
  9.4 78.3 %copy-start.4 = (bf16[6,64,1024]{2,1,0:T(8,128)(2,1)}, bf16[6,64,1024]{2,1,0:T(8,128)(2,1)S(1)}, u32[]{:S(2)}) copy-start(bf16[6,64,1024]{2,1,0:T(8,128)(2,1)S(1)} %get-tuple-element.146.refs_5_) | copy-start | bytes 2359300
  269.1 48.7 %copy-start.10 = (bf16[1,160,1024]{2,1,0:T(8,128)(2,1)S(1)}, bf16[1,160,1024]{2,1,0:T(8,128)(2,1)}, u32[]{:S(2)}) copy-start(bf16[1,160,1024]{2,1,0:T(8,128)(2,1)} %param.17) | copy-start | bytes 983044
  551.8 0.8 copy-start
  552.6 73.6 %copy-start.8 = (f32[16,1024]{1,0:T(8,128)S(1)}, f32[16,1024]{1,0:T(8,128)}, u32[]{:S(2)}) copy-start(f32[16,1024]{1,0:T(8,128)} %get-tuple-element.108) | copy-start | bytes 196612
  552.6 73.6 %copy-start.9 = (f32[16,1024]{1,0:T(8,128)S(1)}, f32[16,1024]{1,0:T(8,128)}, u32[]{:S(2)}) copy-start(f32[16,1024]{1,0:T(8,128)} %get-tuple-element.107) | copy-start | bytes 196612
  552.6 74.9 %copy-start.1 = (f32[6,64,1024]{2,1,0:T(8,128)S(1)}, f32[6,64,1024]{2,1,0:T(8,128)}, u32[]{:S(2)}) copy-start(f32[6,64,1024]{2,1,0:T(8,128)} %get-tuple-element.111) | copy-start | bytes 4718596
  627.5 1.9 copy-start.2

commit v3 on v1

v3 whole, which is shorter than its diff:
```python
import functools

import jax
import jax.numpy as jnp
from jax import lax
from jax.experimental import pallas as pl
from jax.experimental.pallas import tpu as pltpu
from jax.sharding import PartitionSpec as P

HEAD_DIM = 64
EPS = 1e-05
NEG = -30000.0
MESH = pl.DeviceIdType.MESH
PARTS = 6
BF16 = jnp.bfloat16
F32 = jnp.float32


def flip(index, bit):
    size = 2**bit
    return index + size - 2 * size * ((index // size) % 2)


def flip_all(index, bits):
    for bit in bits:
        index = flip(index, bit)
    return index


def subsets(bits):
    found = [()]
    for bit in bits:
        found = found + [entry + (bit,) for entry in found]
    return found


def orders(fsdp_size):
    top = fsdp_size.bit_length() - 1
    bits = list(range(1, top))
    half = len(bits) // 2
    return bits, bits[half:] + bits[:half]


class Link:
    def __init__(self, send_sem, recv_sem):
        self.send_sem, self.recv_sem, self.used, self.sent = send_sem, recv_sem, 0, []

    def push(self, src, dst, device):
        at = self.used
        self.used += 1
        copy = pltpu.make_async_remote_copy(
            src_ref=src,
            dst_ref=dst,
            send_sem=self.send_sem.at[at],
            recv_sem=self.recv_sem.at[at],
            device_id=device,
            device_id_type=MESH,
        )
        copy.start()
        self.sent.append(copy)
        return copy

    def settle(self, copies):
        for copy in copies:
            copy.wait_send()
            self.sent = [other for other in self.sent if other is not copy]

    def drain(self):
        for copy in self.sent:
            copy.wait_send()
        self.sent = []


def greet(fsdp_size, ctx_size, with_tp):
    me, ctx, tp = lax.axis_index("fsdp"), lax.axis_index("ctx"), lax.axis_index("tp")
    barrier = pltpu.get_barrier_semaphore()
    count = 0
    for bit in range(fsdp_size.bit_length() - 1):
        pl.semaphore_signal(
            barrier, inc=1, device_id={"fsdp": flip(me, bit)}, device_id_type=MESH
        )
        count += 1
    if ctx_size > 1:
        pl.semaphore_signal(barrier, inc=1, device_id={"ctx": 1 - ctx}, device_id_type=MESH)
        count += 1
    if with_tp:
        pl.semaphore_signal(barrier, inc=1, device_id={"tp": 1 - tp}, device_id_type=MESH)
        count += 1
    pl.semaphore_wait(barrier, count)


def rows_of(start, rows):
    return pl.ds(pl.multiple_of(start * rows, rows), rows)


def gather_pushes(fsdp_size, ctx_size):
    steps = fsdp_size.bit_length() - 2
    return (ctx_size - 1) + ctx_size * (2**steps - 1) + 2**steps


class Gather:
    def __init__(self, link, ctx_size, own, whole, block, order, local_sem):
        self.link, self.own, self.whole, self.block, self.order = link, own, whole, block, order
        self.ctx_size = ctx_size
        self.me, self.ctx = lax.axis_index("fsdp"), lax.axis_index("ctx")
        self.waits, self.crossed = {}, False
        self.stay = pltpu.make_async_copy(own, self.rows(self.me, self.ctx), local_sem)

    def rows(self, fsdp, ctx):
        return self.whole.at[rows_of(fsdp * self.ctx_size + ctx, self.block)]

    def spread(self, stream, step):
        ctx = self.ctx if stream == 0 else 1 - self.ctx
        bit = self.order[step]
        to = {"fsdp": flip(self.me, bit)}
        copies = []
        for entry in subsets(self.order[:step]):
            place = self.rows(flip_all(self.me, entry), ctx)
            source = self.own if (stream == 0 and not entry) else place
            copies.append(self.link.push(source, place, to))
        self.waits[stream, step] = copies

    def arrive(self, *key):
        for copy in self.waits.pop(key):
            copy.wait_recv()

    def cross(self):
        if not self.crossed:
            self.crossed = True
            self.waits["ctx",] = [
                self.link.push(self.own, self.rows(self.me, self.ctx), {"ctx": 1 - self.ctx})
            ]

    def start(self):
        self.stay.start()
        self.spread(0, 0)

    def next_step(self, stream, step):
        self.arrive(stream, step - 1)
        self.spread(stream, step)

    def other(self):
        self.cross()
        self.arrive("ctx")
        self.spread(1, 0)

    def core(self):
        last = len(self.order) - 1
        for stream in range(self.ctx_size):
            self.arrive(stream, last)
        self.stay.wait()
        both = self.block * self.ctx_size
        copies = []
        for entry in subsets(self.order):
            place = self.whole.at[rows_of(flip_all(self.me, entry), both)]
            copies.append(self.link.push(place, place, {"fsdp": flip(self.me, 0)}))
        self.waits["core",] = copies

    def finish(self):
        self.arrive("core")

    def events(self):
        found = [self.start]
        for step in range(1, len(self.order)):
            found.append(functools.partial(self.next_step, 0, step))
        if self.ctx_size > 1:
            found.append(self.other)
            for step in range(1, len(self.order)):
                found.append(functools.partial(self.next_step, 1, step))
        return found + [self.core, self.finish]


def in_step(first, second):
    def run(one, two):
        one()
        two()

    return [functools.partial(run, one, two) for one, two in zip(first, second)]


class Total:
    def __init__(self, link, fsdp_size, ctx_size, held, arrived):
        self.link, self.held, self.arrived = link, held, arrived
        me, ctx = lax.axis_index("fsdp"), lax.axis_index("ctx")
        self.partners = [{"fsdp": flip(me, bit)} for bit in range(fsdp_size.bit_length() - 1)]
        if ctx_size > 1:
            self.partners.append({"ctx": 1 - ctx})

    def step(self, at):
        if at > 0:
            self.copy.wait_recv()
            self.held[at] = self.held[at - 1] + self.arrived[at - 1]
        if at < len(self.partners):
            self.copy = self.link.push(self.held.at[at], self.arrived.at[at], self.partners[at])

    def events(self):
        return [functools.partial(self.step, at) for at in range(len(self.partners) + 1)]


def dot_nn(left, right):
    return lax.dot_general(left, right, (((1,), (0,)), ((), ())), preferred_element_type=F32)


def dot_nt(left, right):
    return lax.dot_general(left, right, (((1,), (1,)), ((), ())), preferred_element_type=F32)


def dot_tn(left, right):
    return lax.dot_general(left, right, (((0,), (0,)), ((), ())), preferred_element_type=F32)


TILE = 256
ROOT_HALF = 0.7071067811865476
ROOT_TWO_PI = 2.5066282746310002
VECTORS, BIASES, SMALL_ROWS = 6, 3, 16
PACE, SCATTER_PACE = 2, 2
GAIN_A, SHIFT_A, OUT_B, GAIN_B, SHIFT_B, DOWN_B, QV_B, UP_B = range(8)


def lanes(at, count):
    return pl.ds(pl.multiple_of(at * count, count), count)


def standardized(values):
    centered = values - jnp.mean(values, axis=-1, keepdims=True)
    scale = lax.rsqrt(jnp.mean(centered * centered, axis=-1, keepdims=True) + EPS)
    return centered * scale, scale


def send_pieces(link, partial, sent, got, pieces, partner):
    copies = []
    for at in range(pieces):
        sent[at] = partial(at).astype(BF16)
        copies.append(link.push(sent.at[at], got.at[at], partner))
    return copies


def both_halves(copies, sent, got):
    found = []
    for at, copy in enumerate(copies):
        copy.wait_recv()
        found.append(sent[at].astype(F32) + got[at].astype(F32))
    return jnp.concatenate(found, axis=1)


class Stream:
    def __init__(self):
        self.waiting, self.count, self.done = [], 0, set()

    def release(self, group, events, begin, pace=1):
        for place, event in enumerate(events):
            self.waiting.append((begin + place * pace, self.count, group, event))
            self.count += 1
        self.waiting.sort(key=lambda entry: entry[:2])
        self.last = {entry[2]: entry for entry in self.waiting}

    def __call__(self, count):
        for entry in self.waiting[:count]:
            entry[3]()
            if self.last[entry[2]] is entry:
                self.done.add(entry[2])
        self.waiting = self.waiting[count:]

    def need(self, group):
        while group not in self.done:
            self(1)

    def rest(self):
        self(len(self.waiting))


def forward_kernel(ctx_size, fsdp_size, *refs):
    (
        token_ref,
        mask_ref,
        live_ref,
        small_ref,
        bias_ref,
        own_ref,
        out_ref,
        vector_ref,
        stream_ref,
        query_ref,
        kv_out,
        log_total_ref,
        attended_ref,
        mid_ref,
        pre_ref,
        whole_ref,
        held,
        normed,
        hidden,
        kv,
        sent,
        got,
        small_held,
        small_got,
        send_sem,
        recv_sem,
        local_sem,
        load_sem,
        kv_sem,
    ) = refs
    layers, rows, width = stream_ref.shape
    cols = query_ref.shape[2]
    pieces = width // TILE
    pairs = PARTS // 2
    ctx = lax.axis_index("ctx")
    across = {"tp": 1 - lax.axis_index("tp")}
    greet(fsdp_size, ctx_size, True)
    link = Link(send_sem, recv_sem)
    pump = Stream()
    both = orders(fsdp_size)
    small_held[0] = small_ref[...]
    total = Total(link, fsdp_size, ctx_size, small_held, small_got)
    loads, gathers = {}, {}
    for layer in range(layers):
        for pair in range(pairs):
            found = [
                Gather(
                    link,
                    ctx_size,
                    own_ref.at[layer, part],
                    whole_ref.at[layer, part],
                    own_ref.shape[2],
                    both[part % 2],
                    local_sem.at[layer, part],
                )
                for part in (2 * pair, 2 * pair + 1)
            ]
            gathers[layer, pair] = found

            def bring(layer=layer, pair=pair):
                for part in (2 * pair, 2 * pair + 1):
                    copy = pltpu.make_async_copy(
                        whole_ref.at[layer, part],
                        held.at[layer % 2, part],
                        load_sem.at[layer % 2, part],
                    )
                    copy.start()
                    loads[layer, part] = copy

            events = in_step(*[gather.events() for gather in found]) + [bring]
            pump.release((layer, pair), events, PACE * (layer * pairs + pair))

    def cross(layer):
        if layer < layers and ctx_size > 1:
            for pair in range(pairs):
                for gather in gathers[layer, pair]:
                    gather.cross()

    def need(layer, pair):
        pump.need((layer, pair))
        for part in (2 * pair, 2 * pair + 1):
            loads[layer, part].wait()

    total.step(0)
    cross(0)
    for at in range(1, len(total.partners) + 1):
        pump(1)
        total.step(at)
    vector_ref[...] = small_held[len(total.partners)].astype(F32)
    mask = mask_ref[...]
    stream_ref[0] = mask * token_ref[...].astype(F32)
    mine = rows_of(ctx, rows)
    pair_cols = 2 * HEAD_DIM
    lane = lax.broadcasted_iota(jnp.int32, (rows, pair_cols), 1)
    first = lane < HEAD_DIM
    live = live_ref[...] > 0
    kv_saves = []
    log_total_ref[...] = jnp.zeros_like(log_total_ref)

    for layer in range(layers):
        slot = layer % 2

        def vector(which):
            at = layer * VECTORS + which
            return vector_ref[at : at + 1, :]

        def bias(which, at, slot_layer=layer):
            row = slot_layer * BIASES + which
            return bias_ref[row : row + 1, lanes(at, TILE)]

        normal, _ = standardized(stream_ref[layer])
        normed[...] = (normal * vector(GAIN_A) + vector(SHIFT_A)).astype(BF16)
        need(layer, 0)

        @pl.loop(0, cols // TILE)
        def _(at):
            rows_in = normed[...]
            kv[layer, mine, lanes(at, TILE)] = dot_nn(
                rows_in, held[slot, 0, :, lanes(at + cols // TILE, TILE)]
            ).astype(BF16)
            kv[layer, mine, lanes(at + cols // TILE, TILE)] = (
                dot_nn(rows_in, held[slot, 1, :, lanes(at, TILE)])
                + bias(0, at + cols // TILE)
            ).astype(BF16)

        kv_copy = None
        if ctx_size > 1:
            kv_copy = link.push(kv.at[layer, mine], kv.at[layer, mine], {"ctx": 1 - ctx})

        @pl.loop(0, cols // TILE)
        def _(at):
            query_ref[layer, :, lanes(at, TILE)] = (
                dot_nn(normed[...], held[slot, 0, :, lanes(at, TILE)]) + bias(0, at)
            ).astype(BF16)

        pump(3)
        if kv_copy is not None:
            kv_copy.wait_recv()
        cross(layer + 1)
        save = pltpu.make_async_copy(kv.at[layer], kv_out.at[layer], kv_sem.at[layer])
        save.start()
        kv_saves.append(save)

        for half in range(2):
            per_half = cols // pair_cols // 2

            @pl.loop(half * per_half, (half + 1) * per_half)
            def _(at):
                queries = query_ref[layer, :, lanes(at, pair_cols)]
                keys = kv[layer, :, lanes(at, pair_cols)]
                values = kv[layer, :, lanes(at + cols // pair_cols, pair_cols)]
                found = []
                for head in range(2):
                    chosen = jnp.where(
                        first if head == 0 else ~first, queries, jnp.zeros_like(queries)
                    )
                    scores = jnp.where(live, dot_nt(chosen, keys) * HEAD_DIM**-0.5, NEG)
                    top = jnp.max(scores, axis=-1, keepdims=True)
                    weights = jnp.exp(scores - top)
                    summed = jnp.sum(weights, axis=-1, keepdims=True)
                    log_total_ref[layer] = jnp.where(
                        lane == 2 * at + head, top + jnp.log(summed), log_total_ref[layer]
                    )
                    found.append(dot_nn((weights * (1.0 / summed)).astype(BF16), values))
                attended_ref[layer, :, lanes(at, pair_cols)] = jnp.where(
                    first, found[0], found[1]
                ).astype(BF16)

            pump(2)

        def out_partial(at):
            return dot_nt(attended_ref[layer], held[slot, 1, at * TILE : (at + 1) * TILE, cols:])

        copies = send_pieces(link, out_partial, sent.at[layer, 0], got.at[0], pieces, across)
        pump(2)
        branch = both_halves(copies, sent.at[layer, 0], got.at[0])
        mid = stream_ref[layer] + mask * (branch + vector(OUT_B))
        mid_ref[layer] = mid
        normal, _ = standardized(mid)
        normed[...] = (normal * vector(GAIN_B) + vector(SHIFT_B)).astype(BF16)
        need(layer, 1)
        for part in range(2):

            @pl.loop(0, pieces)
            def _(at):
                pre = dot_nn(normed[...], held[slot, 2 + part, :, lanes(at, TILE)]) + bias(
                    1 + part, at
                )
                pre_ref[layer, part, :, lanes(at, TILE)] = pre
                hidden[part, :, lanes(at, TILE)] = (
                    0.5 * pre * (1.0 + lax.erf(pre * ROOT_HALF))
                ).astype(BF16)

            pump(1)
        need(layer, 2)

        def down_partial(at):
            here = slice(at * TILE, (at + 1) * TILE)
            return dot_nt(hidden[0], held[slot, 4, here, :]) + dot_nt(
                hidden[1], held[slot, 5, here, :]
            )

        copies = send_pieces(link, down_partial, sent.at[layer, 1], got.at[1], pieces, across)
        pump(3)
        branch = both_halves(copies, sent.at[layer, 1], got.at[1])
        after = mid_ref[layer] + mask * (branch + vector(DOWN_B))
        if layer + 1 < layers:
            stream_ref[layer + 1] = after
        else:
            out_ref[...] = after.astype(BF16)
    pump.rest()
    link.drain()
    for save in kv_saves:
        save.wait()


def forward_all(mesh, tokens, mask, live, small, biases, own):
    fsdp_size, ctx_size = mesh.shape["fsdp"], mesh.shape["ctx"]
    rows, width = tokens.shape
    layers, _, block, part_cols = own.shape
    cols = width // mesh.shape["tp"]
    slots_all = rows * ctx_size
    pieces = width // TILE
    steps = fsdp_size.bit_length() - 1 + (ctx_size > 1)
    shape = jax.ShapeDtypeStruct
    whole = (layers, PARTS, width, part_cols)
    out_shape = [
        shape((rows, width), BF16),
        shape(small.shape, F32),
        shape((layers, rows, width), F32),
        shape((layers, rows, cols), BF16),
        shape((layers, slots_all, 2 * cols), BF16),
        shape((layers, rows, 2 * HEAD_DIM), F32),
        shape((layers, rows, cols), BF16),
        shape((layers, rows, width), F32),
        shape((layers, 2, rows, width), F32),
        shape(whole, BF16),
    ]
    vmem = pl.BlockSpec(memory_space=pltpu.VMEM)
    any_space = pl.BlockSpec(memory_space=pl.ANY)
    pushes = (
        layers * ((ctx_size > 1) + 2 * pieces + gather_pushes(fsdp_size, ctx_size) * PARTS) + steps
    )
    return pl.pallas_call(
        functools.partial(forward_kernel, ctx_size, fsdp_size),
        out_shape=out_shape,
        in_specs=[vmem] * 5 + [any_space],
        out_specs=[vmem] * 4 + [any_space] + [vmem] * 4 + [any_space],
        scratch_shapes=[
            pltpu.VMEM((2,) + whole[1:], BF16),
            pltpu.VMEM((rows, width), BF16),
            pltpu.VMEM((2, rows, width), BF16),
            pltpu.VMEM((layers, slots_all, 2 * cols), BF16),
            pltpu.VMEM((layers, 2, pieces, rows, TILE), BF16),
            pltpu.VMEM((2, pieces, rows, TILE), BF16),
            pltpu.VMEM((steps + 1,) + small.shape, BF16),
            pltpu.VMEM((steps,) + small.shape, BF16),
            pltpu.SemaphoreType.DMA((pushes,)),
            pltpu.SemaphoreType.DMA((pushes,)),
            pltpu.SemaphoreType.DMA((layers, PARTS)),
            pltpu.SemaphoreType.DMA((2, PARTS)),
            pltpu.SemaphoreType.DMA((layers,)),
        ],
        compiler_params=pltpu.CompilerParams(
            collective_id=0, has_side_effects=True, vmem_limit_bytes=60 * 2**20
        ),
        name="forward_all",
    )(tokens, mask, live, small, biases, own)


class Scatter:
    def __init__(self, link, ctx_size, terms, arrived, last, order, credits, first, final, write):
        self.link, self.terms, self.arrived, self.last = link, terms, arrived, last
        self.ctx_size, self.order, self.write = ctx_size, order, write
        self.credits, self.first, self.final = credits, first, final
        self.me, self.ctx = lax.axis_index("fsdp"), lax.axis_index("ctx")
        self.slots = 2 ** len(order)
        self.both = terms.shape[0] // (2 * self.slots)
        self.flips = [
            [bit for at, bit in enumerate(order) if (slot >> (len(order) - 1 - at)) % 2 == 1]
            for slot in range(self.slots)
        ]
        self.base, self.sent = 0, []

    def place(self, slot, core=0):
        start = flip(self.me, 0) if core else self.me
        return rows_of(flip_all(start, self.flips[slot]), self.both)

    def send(self, step, pieces, to):
        if not self.first:
            pl.semaphore_wait(self.credits.at[step], 1)
        self.copies = [self.link.push(src, dst, to) for src, dst in pieces]
        self.sent += self.copies

    def read(self, step, to):
        if not self.final:
            pl.semaphore_signal(
                self.credits.at[step], inc=1, device_id=to, device_id_type=MESH
            )

    def start(self):
        self.send(
            0,
            [
                (self.terms.at[self.place(slot, 1)], self.arrived.at[slot])
                for slot in range(self.slots)
            ],
            {"fsdp": flip(self.me, 0)},
        )

    def take(self, step, count, to):
        for copy in self.copies:
            copy.wait_recv()
        for slot in range(count):
            here = self.place(slot)
            self.terms[here, :] = self.terms[here, :] + self.arrived[self.base + slot]
        self.base += count
        self.read(step, to)

    def step(self, at):
        count = self.slots >> at
        self.take(at, count, {"fsdp": flip(self.me, 0 if at == 0 else self.order[at - 1])})
        half = count // 2
        self.send(
            at + 1,
            [
                (self.terms.at[self.place(half + slot)], self.arrived.at[self.base + slot])
                for slot in range(half)
            ],
            {"fsdp": flip(self.me, self.order[at])},
        )

    def across(self):
        steps = len(self.order)
        self.take(steps, 1, {"fsdp": flip(self.me, self.order[-1])})
        if self.ctx_size > 1:
            block = self.both // self.ctx_size
            theirs = rows_of(self.me * self.ctx_size + 1 - self.ctx, block)
            self.send(steps + 1, [(self.terms.at[theirs], self.last)], {"ctx": 1 - self.ctx})

    def finish(self):
        block = self.both // self.ctx_size
        total = self.terms[rows_of(self.me * self.ctx_size + self.ctx, block), :].astype(F32)
        if self.ctx_size > 1:
            for copy in self.copies:
                copy.wait_recv()
            total = total + self.last[...].astype(F32)
            self.read(len(self.order) + 1, {"ctx": 1 - self.ctx})
        self.write(total)
        self.link.settle(self.sent)

    def events(self):
        found = [self.start]
        for at in range(len(self.order)):
            found.append(functools.partial(self.step, at))
        return found + [self.across, self.finish]


def norm_pull(normal, scale, gain, grad):
    grad_gain = jnp.sum(grad * normal, axis=0, keepdims=True)
    grad_shift = jnp.sum(grad, axis=0, keepdims=True)
    inner = grad * gain
    along = jnp.mean(inner * normal, axis=-1, keepdims=True)
    grad_in = scale * (inner - jnp.mean(inner, axis=-1, keepdims=True) - normal * along)
    return grad_in, grad_gain, grad_shift


def backward_kernel(ctx_size, fsdp_size, *refs):
    (
        cotangent_ref,
        mask_ref,
        live_ref,
        vector_ref,
        stream_ref,
        query_ref,
        kv_ref,
        log_total_ref,
        attended_ref,
        mid_ref,
        pre_all,
        whole_ref,
        out_ref,
        summed_ref,
        small_ref,
        pre_ref,
        held,
        terms,
        arrived,
        last,
        turned,
        low,
        low_pre,
        hidden,
        grad_att,
        grad_qk,
        grad_kv,
        kv_sent,
        kv_got,
        sent,
        got,
        small_held,
        small_got,
        send_sem,
        recv_sem,
        load_sem,
        pre_sem,
        credits,
    ) = refs
    layers, rows, width = stream_ref.shape
    cols = query_ref.shape[2]
    pieces = width // TILE
    pairs = PARTS // 2
    ctx = lax.axis_index("ctx")
    across = {"tp": 1 - lax.axis_index("tp")}
    loads = {}

    def bring(layer, parts):
        if layer >= 0:
            for part in parts:
                copy = pltpu.make_async_copy(
                    whole_ref.at[layer, part], held.at[part], load_sem.at[part]
                )
                copy.start()
                loads[layer, part] = copy

    def bring_pre(layer):
        if layer >= 0:
            copy = pltpu.make_async_copy(
                pre_all.at[layer], pre_ref.at[layer % 2], pre_sem.at[layer % 2]
            )
            copy.start()
            loads[layer, "pre"] = copy

    bring_pre(layers - 1)
    bring(layers - 1, (4, 5, 2, 3, 1, 0))
    small_held[...] = jnp.zeros_like(small_held)
    greet(fsdp_size, ctx_size, True)
    link = Link(send_sem, recv_sem)
    pump = Stream()
    both = [order[::-1] for order in orders(fsdp_size)]
    mask = mask_ref[...]
    pair_cols = 2 * HEAD_DIM
    lane = lax.broadcasted_iota(jnp.int32, (rows, pair_cols), 1)
    first = lane < HEAD_DIM
    live = live_ref[...] > 0
    mine, theirs = rows_of(ctx, rows), rows_of(1 - ctx, rows)
    groups = 0
    last_sent = {}

    def scatter(layer, pair):
        nonlocal groups

        def writer(part):
            def write(value):
                summed_ref[layer, part] = value

            return write

        events = in_step(
            *[
                Scatter(
                    link,
                    ctx_size,
                    terms.at[part],
                    arrived.at[part],
                    last.at[part],
                    both[part % 2],
                    credits.at[part],
                    layer == layers - 1,
                    layer == 0,
                    writer(part),
                ).events()
                for part in (2 * pair, 2 * pair + 1)
            ]
        )
        pump.release((layer, pair), events, SCATTER_PACE * groups)
        groups += 1

    def free(layer, pair):
        if layer < layers - 1:
            pump.need((layer + 1, pair))

    def product(part, start, count, right):
        @pl.loop(0, count)
        def _(at):
            terms[part, :, lanes(at + start, TILE)] = dot_nn(turned[...], right(at)).astype(BF16)

    out_ref[...] = cotangent_ref[...].astype(F32)
    for layer in reversed(range(layers)):
        rows_small = small_held.at[layer, 0]

        def vector(which):
            at = layer * VECTORS + which
            return vector_ref[at : at + 1, :]

        def keep_row(which, value):
            rows_small[which : which + 1, :] = value

        bring_pre(layer - 1)
        grad = out_ref[...]
        masked = mask * grad
        keep_row(DOWN_B, jnp.sum(masked, axis=0, keepdims=True))
        low[...] = masked.astype(BF16)
        turned[...] = jnp.transpose(low[...])
        loads[layer, "pre"].wait()
        for part in range(2):
            loads[layer, 4 + part].wait()

            @pl.loop(0, pieces)
            def _(at):
                pre = pre_ref[layer % 2, part, :, lanes(at, TILE)]
                chance = 0.5 * (1.0 + lax.erf(pre * ROOT_HALF))
                hidden[part, :, lanes(at, TILE)] = (pre * chance).astype(BF16)
                slope = chance + pre * (jnp.exp(-0.5 * pre * pre) * (1.0 / ROOT_TWO_PI))
                grad_pre = dot_nn(low[...], held[4 + part, :, lanes(at, TILE)]) * slope
                rows_small[UP_B + part : UP_B + part + 1, lanes(at, TILE)] = jnp.sum(
                    grad_pre, axis=0, keepdims=True
                )
                low_pre[part, :, lanes(at, TILE)] = grad_pre.astype(BF16)

            pump(1)
        bring(layer - 1, (4, 5))
        for part in (2, 3):
            loads[layer, part].wait()

        def up_partial(at):
            here = slice(at * TILE, (at + 1) * TILE)
            return dot_nt(low_pre[0], held[2, here, :]) + dot_nt(low_pre[1], held[3, here, :])

        if layer < layers - 1:
            link.settle(last_sent["up"])
        copies = send_pieces(link, up_partial, sent.at[0], got.at[0], pieces, across)
        last_sent["up"] = copies
        bring(layer - 1, (2, 3))
        free(layer, 2)
        for part in range(2):
            product(4 + part, 0, pieces, lambda at, part=part: hidden[part, :, lanes(at, TILE)])
        scatter(layer, 2)
        pump(1)
        normal, scale = standardized(mid_ref[layer])
        turned[...] = jnp.transpose(
            (normal * vector(GAIN_B) + vector(SHIFT_B)).astype(BF16)
        )
        free(layer, 1)
        for part in range(2):
            product(2 + part, 0, pieces, lambda at, part=part: low_pre[part, :, lanes(at, TILE)])
        scatter(layer, 1)
        pump(1)
        grad_normed = both_halves(copies, sent.at[0], got.at[0])
        normal, scale = standardized(mid_ref[layer])
        grad_in, grad_gain, grad_shift = norm_pull(normal, scale, vector(GAIN_B), grad_normed)
        keep_row(GAIN_B, grad_gain)
        keep_row(SHIFT_B, grad_shift)
        grad_mid = out_ref[...] + grad_in
        out_ref[...] = grad_mid
        masked = mask * grad_mid
        keep_row(OUT_B, jnp.sum(masked, axis=0, keepdims=True))
        low[...] = masked.astype(BF16)
        loads[layer, 1].wait()

        @pl.loop(0, cols // TILE)
        def _(at):
            grad_att[:, lanes(at, TILE)] = dot_nn(
                low[...], held[1, :, lanes(at + cols // TILE, TILE)]
            ).astype(BF16)

        pump(1)
        for half in range(2):
            per_half = cols // pair_cols // 2

            @pl.loop(half * per_half, (half + 1) * per_half)
            def _(at):
                queries = query_ref[layer, :, lanes(at, pair_cols)]
                grads = grad_att[:, lanes(at, pair_cols)]
                keys = kv_ref[layer, :, lanes(at, pair_cols)]
                values = kv_ref[layer, :, lanes(at + cols // pair_cols, pair_cols)]
                found, key_grad, value_grad = [], None, None
                for head in range(2):
                    here = first if head == 0 else ~first
                    query = jnp.where(here, queries, jnp.zeros_like(queries))
                    one_grad = jnp.where(here, grads, jnp.zeros_like(grads))
                    scores = jnp.where(live, dot_nt(query, keys) * HEAD_DIM**-0.5, NEG)
                    log_total = jnp.sum(
                        jnp.where(lane == 2 * at + head, log_total_ref[layer], 0.0),
                        axis=-1,
                        keepdims=True,
                    )
                    weights = jnp.exp(scores - log_total)
                    grad_weights = dot_nt(one_grad, values)
                    along = jnp.sum(weights * grad_weights, axis=-1, keepdims=True)
                    grad_scores = (weights * (grad_weights - along)).astype(BF16)
                    found.append(dot_nn(grad_scores, keys))
                    one = dot_tn(grad_scores, query)
                    two = dot_tn(weights.astype(BF16), one_grad)
                    key_grad = one if head == 0 else key_grad + one
                    value_grad = two if head == 0 else value_grad + two
                grad_qk[:, lanes(at, pair_cols)] = (
                    jnp.where(first, found[0], found[1]) * HEAD_DIM**-0.5
                ).astype(BF16)
                grad_kv[:, lanes(at, pair_cols)] = key_grad * HEAD_DIM**-0.5
                grad_kv[:, lanes(at + cols // pair_cols, pair_cols)] = value_grad

            pump(2)
        kv_copy = None
        if ctx_size > 1:
            if layer < layers - 1:
                link.settle([last_sent["kv"]])
            kv_sent[...] = grad_kv[theirs, :].astype(BF16)
            kv_copy = link.push(kv_sent, kv_got.at[layer], {"ctx": 1 - ctx})
            last_sent["kv"] = kv_copy
        free(layer, 0)
        turned[...] = jnp.transpose(low[...])
        product(1, cols // TILE, cols // TILE, lambda at: attended_ref[layer, :, lanes(at, TILE)])
        normal, scale = standardized(stream_ref[layer])
        turned[...] = jnp.transpose(
            (normal * vector(GAIN_A) + vector(SHIFT_A)).astype(BF16)
        )
        product(0, 0, cols // TILE, lambda at: grad_qk[:, lanes(at, TILE)])
        pump(2)
        total_kv = grad_kv[mine, :]
        if kv_copy is not None:
            kv_copy.wait_recv()
            total_kv = total_kv + kv_got[layer].astype(F32)
        grad_qk[:, cols:] = total_kv.astype(BF16)
        rows_small[QV_B : QV_B + 1, :cols] = jnp.sum(
            grad_qk[:, :cols].astype(F32), axis=0, keepdims=True
        )
        rows_small[QV_B : QV_B + 1, cols:] = jnp.sum(
            grad_qk[:, 2 * cols :].astype(F32), axis=0, keepdims=True
        )
        loads[layer, 0].wait()

        def in_partial(at):
            here = slice(at * TILE, (at + 1) * TILE)
            return dot_nt(grad_qk[:, : 2 * cols], held[0, here, :]) + dot_nt(
                grad_qk[:, 2 * cols :], held[1, here, :cols]
            )

        if layer < layers - 1:
            link.settle(last_sent["in"])
        copies = send_pieces(link, in_partial, sent.at[1], got.at[1], pieces, across)
        last_sent["in"] = copies
        bring(layer - 1, (1, 0))
        product(
            0, cols // TILE, cols // TILE, lambda at: grad_qk[:, lanes(at + cols // TILE, TILE)]
        )
        product(1, 0, cols // TILE, lambda at: grad_qk[:, lanes(at + 2 * cols // TILE, TILE)])
        scatter(layer, 0)
        pump(2)
        grad_normed = both_halves(copies, sent.at[1], got.at[1])
        normal, scale = standardized(stream_ref[layer])
        grad_in, grad_gain, grad_shift = norm_pull(normal, scale, vector(GAIN_A), grad_normed)
        keep_row(GAIN_A, grad_gain)
        keep_row(SHIFT_A, grad_shift)
        grad = out_ref[...] + grad_in
        out_ref[...] = grad if layer > 0 else mask * grad
        total = Total(link, fsdp_size, ctx_size, small_held.at[layer], small_got.at[layer])
        pump.release(("small", layer), total.events(), SCATTER_PACE * (groups - 1))
    pump.rest()
    for layer in range(layers):
        small_ref[layer] = small_held[layer, small_held.shape[1] - 1]
    link.drain()


def backward_all(mesh, cotangent, mask, live, vectors, kept, whole):
    fsdp_size, ctx_size = mesh.shape["fsdp"], mesh.shape["ctx"]
    rows, width = cotangent.shape
    layers, _, _, part_cols = whole.shape
    cols = width // mesh.shape["tp"]
    slots_all = rows * ctx_size
    pieces = width // TILE
    slots = fsdp_size // 2
    both = width // fsdp_size
    block = both // ctx_size
    bits = fsdp_size.bit_length() - 1
    steps = bits + (ctx_size > 1)
    shape = jax.ShapeDtypeStruct
    vmem = pl.BlockSpec(memory_space=pltpu.VMEM)
    any_space = pl.BlockSpec(memory_space=pl.ANY)
    operands = [cotangent, mask, live, vectors, *kept, whole]
    pushes = layers * ((ctx_size > 1) + 2 * pieces + PARTS * (2 * slots) + steps)
    return pl.pallas_call(
        functools.partial(backward_kernel, ctx_size, fsdp_size),
        out_shape=[
            shape((rows, width), F32),
            shape((layers, PARTS, block, part_cols), F32),
            shape((layers, SMALL_ROWS, width), F32),
        ],
        in_specs=[vmem] * (len(operands) - 2) + [any_space] * 2,
        out_specs=[vmem] * 3,
        scratch_shapes=[
            pltpu.VMEM((2, 2, rows, width), F32),
            pltpu.VMEM(whole.shape[1:], BF16),
            pltpu.VMEM(whole.shape[1:], BF16),
            pltpu.VMEM((PARTS, 2 * slots - 1, both, part_cols), BF16),
            pltpu.VMEM((PARTS, block, part_cols), BF16),
            pltpu.VMEM((width, rows), BF16),
            pltpu.VMEM((rows, width), BF16),
            pltpu.VMEM((2, rows, width), BF16),
            pltpu.VMEM((2, rows, width), BF16),
            pltpu.VMEM((rows, cols), BF16),
            pltpu.VMEM((rows, 3 * cols), BF16),
            pltpu.VMEM((slots_all, 2 * cols), F32),
            pltpu.VMEM((rows, 2 * cols), BF16),
            pltpu.VMEM((layers, rows, 2 * cols), BF16),
            pltpu.VMEM((2, pieces, rows, TILE), BF16),
            pltpu.VMEM((2, pieces, rows, TILE), BF16),
            pltpu.VMEM((layers, steps + 1, SMALL_ROWS, width), F32),
            pltpu.VMEM((layers, steps, SMALL_ROWS, width), F32),
            pltpu.SemaphoreType.DMA((pushes,)),
            pltpu.SemaphoreType.DMA((pushes,)),
            pltpu.SemaphoreType.DMA((PARTS,)),
            pltpu.SemaphoreType.DMA((2,)),
            pltpu.SemaphoreType.REGULAR((PARTS, steps + 1)),
        ],
        compiler_params=pltpu.CompilerParams(
            collective_id=1, has_side_effects=True, vmem_limit_bytes=63 * 2**20
        ),
        name="backward_all",
    )(*operands)


def body(
    mesh,
    tokens,
    lengths,
    cotangent,
    attn_gain,
    attn_shift,
    qkv_weight,
    qv_bias,
    out_weight,
    out_bias,
    mlp_gain,
    mlp_shift,
    up_weight,
    up_bias,
    down_weight,
    down_bias,
):
    images, local_slots, width = tokens.shape
    ctx_size = mesh.shape["ctx"]
    rows_here, slots_all = images * local_slots, local_slots * ctx_size
    layers, block, _, cols = qkv_weight.shape
    units = up_weight.shape[2]
    slot_ids = lax.axis_index("ctx") * local_slots + jnp.arange(local_slots, dtype=jnp.int32)
    mask = (slot_ids[None, :] < lengths[:, None]).astype(F32).reshape(rows_here, 1)
    live = (jnp.arange(slots_all, dtype=jnp.int32)[None, :] < lengths[:, None]).astype(F32)
    vectors = jnp.stack((attn_gain, attn_shift, out_bias, mlp_gain, mlp_shift, down_bias), axis=1)
    vectors = vectors.reshape(layers * VECTORS, block)
    here = (lax.axis_index("fsdp") * ctx_size + lax.axis_index("ctx")) * block
    small = lax.dynamic_update_slice(
        jnp.zeros((-(-vectors.shape[0] // 16) * 16, width), BF16), vectors, (0, here)
    )
    biases = jnp.concatenate(
        (qv_bias.reshape(layers, 1, width), up_bias.reshape(layers, units // width, width)), axis=1
    ).reshape(layers * BIASES, width)
    biases = jnp.pad(biases.astype(F32), ((0, -biases.shape[0] % 8), (0, 0)))
    out_t = jnp.swapaxes(out_weight, 1, 2)
    down_t = jnp.swapaxes(down_weight, 1, 2)
    own = jnp.stack(
        (
            qkv_weight[:, :, 0:2].reshape(layers, block, 2 * cols),
            jnp.concatenate((qkv_weight[:, :, 2], out_t), axis=2),
            up_weight[:, :, : units // 2],
            up_weight[:, :, units // 2 :],
            down_t[:, :, : units // 2],
            down_t[:, :, units // 2 :],
        ),
        axis=1,
    )
    found = forward_all(
        mesh, tokens.reshape(rows_here, width), mask, live, small, biases, own
    )
    output, vectors, *kept, whole = found
    output = output.reshape(tokens.shape)
    grad, big, little = backward_all(
        mesh, cotangent.reshape(rows_here, width), mask, live, vectors, kept, whole
    )
    input_grad = grad.reshape(tokens.shape)
    own_vectors = lax.dynamic_slice_in_dim(little[:, :6], here, block, axis=2)
    grad_qkv = jnp.concatenate((big[:, 0], big[:, 1, :, :cols]), axis=2)
    return (
        output,
        input_grad,
        own_vectors[:, 0],
        own_vectors[:, 1],
        grad_qkv.reshape(layers, block, 3, cols),
        little[:, 6].reshape(layers, 2, cols),
        jnp.swapaxes(big[:, 1, :, cols:], 1, 2),
        own_vectors[:, 2],
        own_vectors[:, 3],
        own_vectors[:, 4],
        jnp.concatenate((big[:, 2], big[:, 3]), axis=2),
        little[:, 7 : 7 + units // width].reshape(layers, units),
        jnp.swapaxes(jnp.concatenate((big[:, 4], big[:, 5]), axis=2), 1, 2),
        own_vectors[:, 5],
    )


def solution(mesh):
    place = P(None, ("fsdp", "ctx"))
    rows = P("fsdp", "ctx", None)
    return jax.shard_map(
        functools.partial(body, mesh),
        mesh=mesh,
        in_specs=(
            rows,
            P("fsdp"),
            rows,
            place,
            place,
            P(None, ("fsdp", "ctx"), None, "tp"),
            P(None, None, "tp"),
            P(None, "tp", ("fsdp", "ctx")),
            place,
            place,
            place,
            P(None, ("fsdp", "ctx"), "tp"),
            P(None, "tp"),
            P(None, "tp", ("fsdp", "ctx")),
            place,
        ),
        out_specs=(
            rows,
            rows,
            place,
            place,
            P(None, ("fsdp", "ctx"), None, "tp"),
            P(None, None, "tp"),
            P(None, "tp", ("fsdp", "ctx")),
            place,
            place,
            place,
            P(None, ("fsdp", "ctx"), "tp"),
            P(None, "tp"),
            P(None, "tp", ("fsdp", "ctx")),
            place,
        ),
        check_vma=False,
    )
```

time: 2480 us -> 565 us (0.23)
  blocking collectives: 1450 us -> 0 us
  waiting for transfers between devices: 242 us -> 0 us
  matrix products: 182 us -> 0 us
  Pallas kernels: 433 us -> 527 us
  other arithmetic: 82.2 us -> 3.95 us
  local copies, waits for them, and re-layouts: 60.3 us -> 24.2 us
    unnamed x3 -> x0, blocking collectives: 1400 us -> none
    psum x11 -> x0, waiting for transfers between devices: 241 us -> none  [head_sum(): return lax.psum(partial_rows, 'tp')]
    dot_general x84 -> x0, matrix products: 182 us -> none  [dot(): return jnp.einsum(spec, left, right, preferred_element_type=F32)]
    pallas_call x6 -> x2, Pallas kernels: 433 us -> 527 us  [the longest x1 279 us: backward_all(): pl.pallas_call(functools.partial(backward_kernel, ctx_size, fsdp_size), o...]
    all_gather x3 -> x0, blocking collectives: 48.8 us -> none  [body(): lax.all_gather(jnp.concatenate((keys_own, values_own), -1), 'ctx', axis=1...]
    reduce_sum x33 -> x0, other arithmetic: 37.5 us -> none  [the longest x6 12.4 us: layer_norm(): return centered * lax.rsqrt(row_var + EPS) * norm_gain + norm_shift]
  transfers between devices with their start and end apart: 11 -> 0, of which waited for: 9 -> 0; matrix products, arithmetic and copies ran while one was open for 2% -> 0% of each run, Pallas kernels for 5% -> 0%
where the time goes in v3:
time: 565 us; the launch traced here: 557 us
  Pallas kernels  527 us (93%)
  local copies, waits for them, and re-layouts  24.2 us (4%)
    pallas_call x1, Pallas kernels, backward_all(): pl.pallas_call(functools.partial(backward_kernel, ctx_size, fsdp_size), o...  279 us
    pallas_call x1, Pallas kernels, forward_all(): pl.pallas_call(functools.partial(forward_kernel, ctx_size, fsdp_size), ou...  247 us

profile of v3, /device:TPU:0, one launch (start us, length us, event | category | flops | bytes accessed | tf_op | source)
XLA Modules:
  0.0 556.9 jit_solution(16884249518037706388)
XLA Ops:
  1.3 0.7 fusion.3.refs_1_
  2.0 0.6 compare_convert_fusion.refs_2_
  2.6 0.7 constant_dynamic-update-slice_fusion.5
  3.2 0.7 constant_dynamic-update-slice_fusion.4
  3.9 0.7 constant_dynamic-update-slice_fusion.3
  4.6 0.7 constant_dynamic-update-slice_fusion.2
  5.3 0.7 constant_dynamic-update-slice_fusion.1
  6.0 0.7 constant_dynamic-update-slice_fusion
  6.7 0.5 dynamic_update_slice.3.refs_3_
  7.3 0.8 reshape.94
  8.0 0.7 reshape.100
  8.8 0.6 pad_convert_fusion.refs_4_
  9.4 1.0 slice.66
  11.2 1.0 slice_bitcast_fusion.9
  12.5 1.4 copy-done
  13.8 247.5 %forward_all.1 = (bf16[160,1024]{1,0:T(8,128)(2,1)}, f32[32,1024]{1,0:T(8,128)}, f32[3,160,1024]{2,1,0:T(8,128)}, bf16[3,160,512]{2,1,0:T(8,128)(2,1)}, bf16[3,3...) custom-call(bf16[160,1024]{1,0:T(8,128)(2,1)} %bitcast.86, ...), custom_call_target="tpu_custom_call" | custom-call | tf_op jit(solution)/shard_map/forward_all/pallas_call | solution.py:517
  261.3 279.3 %backward_all.1 = (f32[160,1024]{1,0:T(8,128)}, f32[3,6,64,1024]{3,2,1,0:T(8,128)}, f32[3,16,1024]{2,1,0:T(8,128)}) custom-call(bf16[160,1024]{1,0:T(8,128)(2,1)} %bitcast.85, f32[160,1]{1,0:T(8,128)} %fusion.3.refs_1_, f32[1,320]{1,0:T(1,128)} %compare_convert_fusion.refs_2_, f32[32,1024]{1,0:T(8,128)} %get-tuple-element.28.refs_3_, ...), custom_call_target="tpu_custom_call" | custom-call | tf_op jit(solution)/shard_map/backward_all/pallas_call | solution.py:955
  540.6 0.9 slice.72
  541.6 0.6 copy_bitcast_fusion.5
  542.2 1.9 slice_bitcast_fusion.7
  544.1 1.8 slice_bitcast_fusion.2
  546.0 1.1 copy.63
  547.1 0.9 slice_reduce_fusion
  548.0 0.6 reshape_squeeze.3
  548.7 0.6 copy_bitcast_fusion.3
  549.2 0.6 copy_bitcast_fusion.1
  549.8 1.5 slice_bitcast_fusion
  551.4 1.9 pad_maximum_fusion
  553.3 0.9 slice_bitcast_fusion.10
  554.3 0.6 copy.53
  554.9 0.7 copy.78
  555.6 0.8 copy.79
  (28 shorter events, 1.2 us)
Async XLA Ops:
  0.6 11.6 %copy-start.6 = (bf16[3,512,64]{1,2,0:T(8,128)(2,1)S(1)}, bf16[3,512,64]{1,2,0:T(8,128)(2,1)}, u32[]{:S(2)}) copy-start(bf16[3,512,64]{1,2,0:T(8,128)(2,1)} %param.22) | copy-start | bytes 589828
  2.0 10.3 %copy-start.1 = (bf16[3,64,2048]{2,1,0:T(8,128)(2,1)S(1)}, bf16[3,64,2048]{2,1,0:T(8,128)(2,1)}, u32[]{:S(2)}) copy-start(bf16[3,64,2048]{2,1,0:T(8,128)(2,1)} %param.26) | copy-start | bytes 2359300
  7.3 5.1 copy-start.5
  11.2 1.2 copy-start.2
  12.5 1.4 copy-start
  551.4 3.5 copy-start.4
  551.4 4.3 copy-start.3
